TPU v7x, 256 devices: a whole 4x4x8 slice. The times are simulated.
256 devices in a mesh: dp: 32 (over z_lo, x, y), ctx: 8 (over z_hi, core).
Axes of the slice: x: 4, y: 4, z: 8 (z_hi: 4, z_lo: 2; z = z_hi * 2 + z_lo), core: 2. Of those that a mesh axis runs over, the one named last changes fastest.
Arguments:
- tokens: bfloat16 [2, 32768, 576], P(None, ('dp', 'ctx')), may hold values from -6 to 6
- lengths: int32 [2, 32, 4], P(None, 'dp'), may hold values from 1 to 1021, as said below
- gain_attn: bfloat16 [576], P('dp'), may hold values from 0.25 to 1.75
- w_query: bfloat16 [576, 576], P('dp', 'ctx'), may hold values from -0.25 to 0.25
- w_key: bfloat16 [576, 192], P('dp', 'ctx'), may hold values from -0.25 to 0.25
- w_value: bfloat16 [576, 192], P('dp', 'ctx'), may hold values from -0.25 to 0.25
- w_out: bfloat16 [576, 576], P('dp', 'ctx'), may hold values from -3.5 to 3.5
- gain_ffn: bfloat16 [576], P('dp'), may hold values from 0.25 to 1.75
- w_gate: bfloat16 [576, 1536], P('dp', 'ctx'), may hold values from -0.25 to 0.25
- w_up: bfloat16 [576, 1536], P('dp', 'ctx'), may hold values from -0.25 to 0.25
- w_down: bfloat16 [1536, 576], P('dp', 'ctx'), may hold values from -0.15625 to 0.15625
- cotangent: bfloat16 [2, 32768, 576], P(None, ('dp', 'ctx')), may hold values from -6 to 6
Outputs:
- block_out: bfloat16 [2, 32768, 576], P(None, ('dp', 'ctx'))
- d_tokens: float32 [2, 32768, 576], P(None, ('dp', 'ctx'))
- grad_gain_attn: float32 [576], P('dp')
- grad_query: float32 [576, 576], P('dp', 'ctx')
- grad_key: float32 [576, 192], P('dp', 'ctx')
- grad_value: float32 [576, 192], P('dp', 'ctx')
- grad_out: float32 [576, 576], P('dp', 'ctx')
- grad_gain_ffn: float32 [576], P('dp')
- grad_gate: float32 [576, 1536], P('dp', 'ctx')
- grad_up: float32 [576, 1536], P('dp', 'ctx')
- grad_down: float32 [1536, 576], P('dp', 'ctx')
Inputs may be any that keep to these rules, and one draw needn't show every extreme that they name: The 4 lengths of each row sum to 1024; one of them, at a place drawn from the seed, is longer than 896. In the first row of the first micro-batch the other documents have one token each.
All inputs are finite; a program needn't handle non-finite values.
Results may differ from a plain program's by a relative error of at most 0.03.
Values may be sent and summed in bfloat16 or wider, within the bound.
No kernel may reach another device: no remote copies, remote signals or barrier semaphores. Data moves between devices by JAX's collectives and lax.ppermute only.
A program may use at most 128 MiB of HBM per device.

v0:
```python
import jax
import jax.numpy as jnp
from jax import lax
from jax.sharding import PartitionSpec as P

HEADS = 9
KV_HEADS = 3
HEAD = 64


EPSILON = 1e-05
ROPE_BASE = 100000.0
MASKED = -1e30


def dot_low(first_op, second_op):
    return jnp.dot(first_op, second_op, preferred_element_type=jnp.float32)


def dot_first(first_op, second_op):
    return lax.dot_general(
        first_op, second_op, (((0,), (0,)), ((), ())), preferred_element_type=jnp.float32
    )


def dot_second(first_op, second_op):
    return lax.dot_general(
        first_op, second_op, (((1,), (1,)), ((), ())), preferred_element_type=jnp.float32
    )


def rms_scale(values):
    return lax.rsqrt(jnp.mean(values * values, axis=-1, keepdims=True) + EPSILON)


def doc_layout(doc_sizes, places):
    doc_ends = jnp.cumsum(doc_sizes)
    passed = places[:, None] >= doc_ends[None, :]
    segment = jnp.sum(passed.astype(jnp.int32), axis=1)
    before = jnp.sum(jnp.where(passed, doc_sizes[None, :], 0), axis=1)
    return (segment, places - before)


def rotary(positions):
    half_size = HEAD // 2
    frequencies = ROPE_BASE ** (-jnp.arange(half_size, dtype=jnp.float32) / half_size)
    angles = positions.astype(jnp.float32)[:, None] * frequencies[None, :]
    angles = jnp.concatenate([angles, angles], axis=1)
    return (jnp.cos(angles), jnp.sin(angles))


def turned(values):
    half_size = values.shape[-1] // 2
    return jnp.concatenate([-values[..., half_size:], values[..., :half_size]], axis=-1)


def rotate(values, cosine, sine_table):
    return values * cosine[:, None, :] + turned(values) * sine_table[:, None, :]


def unrotate(values, cosine, sine_table):
    return values * cosine[:, None, :] - turned(values) * sine_table[:, None, :]


def fetch_weights(shards):
    widened = (
        lax.all_gather(shards[0], "ctx", axis=1, tiled=True),
        lax.all_gather(shards[1], "ctx", axis=1, tiled=True),
        lax.all_gather(shards[2], "ctx", axis=1, tiled=True),
        lax.all_gather(shards[3], "ctx", axis=1, tiled=True),
        lax.all_gather(shards[4], "ctx", axis=1, tiled=True),
        lax.all_gather(shards[5], "ctx", axis=1, tiled=True),
        lax.all_gather(shards[6], "ctx", axis=1, tiled=True),
    )
    return (
        lax.all_gather(widened[0], "dp", axis=0, tiled=True),
        lax.all_gather(widened[1], "dp", axis=0, tiled=True),
        lax.all_gather(widened[2], "dp", axis=0, tiled=True),
        lax.all_gather(widened[3], "dp", axis=0, tiled=True),
        lax.all_gather(widened[4], "dp", axis=0, tiled=True),
        lax.all_gather(widened[5], "dp", axis=0, tiled=True),
        lax.all_gather(widened[6], "dp", axis=0, tiled=True),
        lax.all_gather(shards[7], "dp", axis=0, tiled=True),
        lax.all_gather(shards[8], "dp", axis=0, tiled=True),
    )


def reduce_grads(gradients, ctx_count):
    owned = (
        lax.psum_scatter(
            gradients[0].astype(jnp.bfloat16), "dp", scatter_dimension=0, tiled=True
        ).astype(jnp.float32),
        lax.psum_scatter(
            gradients[1].astype(jnp.bfloat16), "dp", scatter_dimension=0, tiled=True
        ).astype(jnp.float32),
        lax.psum_scatter(
            gradients[2].astype(jnp.bfloat16), "dp", scatter_dimension=0, tiled=True
        ).astype(jnp.float32),
        lax.psum_scatter(
            gradients[3].astype(jnp.bfloat16), "dp", scatter_dimension=0, tiled=True
        ).astype(jnp.float32),
        lax.psum_scatter(
            gradients[4].astype(jnp.bfloat16), "dp", scatter_dimension=0, tiled=True
        ).astype(jnp.float32),
        lax.psum_scatter(
            gradients[5].astype(jnp.bfloat16), "dp", scatter_dimension=0, tiled=True
        ).astype(jnp.float32),
        lax.psum_scatter(
            gradients[6].astype(jnp.bfloat16), "dp", scatter_dimension=0, tiled=True
        ).astype(jnp.float32),
        lax.psum_scatter(
            gradients[7].astype(jnp.bfloat16), "dp", scatter_dimension=0, tiled=True
        ).astype(jnp.float32),
        lax.psum_scatter(
            gradients[8].astype(jnp.bfloat16), "dp", scatter_dimension=0, tiled=True
        ).astype(jnp.float32),
    )
    gain_pair = jnp.stack([owned[7], owned[8]], axis=0)
    spread = jnp.broadcast_to(gain_pair[None], (ctx_count,) + gain_pair.shape)
    final = (
        lax.psum_scatter(
            owned[0].astype(jnp.bfloat16), "ctx", scatter_dimension=1, tiled=True
        ).astype(jnp.float32),
        lax.psum_scatter(
            owned[1].astype(jnp.bfloat16), "ctx", scatter_dimension=1, tiled=True
        ).astype(jnp.float32),
        lax.psum_scatter(
            owned[2].astype(jnp.bfloat16), "ctx", scatter_dimension=1, tiled=True
        ).astype(jnp.float32),
        lax.psum_scatter(
            owned[3].astype(jnp.bfloat16), "ctx", scatter_dimension=1, tiled=True
        ).astype(jnp.float32),
        lax.psum_scatter(
            owned[4].astype(jnp.bfloat16), "ctx", scatter_dimension=1, tiled=True
        ).astype(jnp.float32),
        lax.psum_scatter(
            owned[5].astype(jnp.bfloat16), "ctx", scatter_dimension=1, tiled=True
        ).astype(jnp.float32),
        lax.psum_scatter(
            owned[6].astype(jnp.bfloat16), "ctx", scatter_dimension=1, tiled=True
        ).astype(jnp.float32),
        lax.psum_scatter(
            spread.astype(jnp.bfloat16), "ctx", scatter_dimension=0, tiled=True
        ).astype(jnp.float32),
    )
    return (
        final[0],
        final[1],
        final[2],
        final[3],
        final[4],
        final[5],
        final[6],
        final[7][0, 0],
        final[7][0, 1],
    )


def piece_mask(piece, doc_sizes, segment, places):
    kv_width = KV_HEADS * HEAD
    key_count = piece.shape[0]
    key_rows = piece[:, :kv_width].reshape(key_count, KV_HEADS, HEAD)
    value_rows = piece[:, kv_width:].reshape(key_count, KV_HEADS, HEAD)
    key_places = jnp.arange(key_count, dtype=jnp.int32)
    key_segment, key_positions = doc_layout(doc_sizes, key_places)
    allowed = (segment[:, None] == key_segment[None, :]) & (key_places[None, :] <= places[:, None])
    return (key_rows, value_rows, allowed)


def attention_forward(q_heads, pairs, doc_sizes, segment, places):
    row_count = q_heads.shape[0]
    groups = HEADS // KV_HEADS
    score_scale = HEAD ** (-0.5)
    running = jnp.full((KV_HEADS, groups, row_count), MASKED, jnp.float32)
    key_rows, value_rows, allowed = piece_mask(
        lax.all_gather(pairs, "ctx", axis=0, tiled=True), doc_sizes, segment, places
    )
    scores = (
        jnp.einsum("qkgd,skd->kgqs", q_heads, key_rows, preferred_element_type=jnp.float32)
        * score_scale
    )
    scores = jnp.where(allowed, scores, MASKED)
    highest = jnp.maximum(running, jnp.max(scores, axis=-1))
    weights = jnp.where(allowed, jnp.exp(scores - highest[..., None]), 0.0)
    totals = jnp.sum(weights, axis=-1)
    accum = jnp.einsum(
        "kgqs,skd->kgqd",
        weights.astype(jnp.bfloat16),
        value_rows,
        preferred_element_type=jnp.float32,
    )
    running, totals, accum = (highest, totals, accum)
    mixture = accum / totals[..., None]
    attended = jnp.transpose(mixture, (2, 0, 1, 3)).reshape(row_count, HEADS * HEAD)
    return (attended, running + jnp.log(totals))


def attention_backward(q_heads, pairs, doc_sizes, segment, places, log_total, d_heads, delta):
    kv_width = KV_HEADS * HEAD
    score_scale = HEAD ** (-0.5)
    piece = lax.all_gather(pairs, "ctx", axis=0, tiled=True)
    key_count = piece.shape[0]
    key_rows, value_rows, allowed = piece_mask(piece, doc_sizes, segment, places)
    scores = (
        jnp.einsum("qkgd,skd->kgqs", q_heads, key_rows, preferred_element_type=jnp.float32)
        * score_scale
    )
    probabilities = jnp.where(allowed, jnp.exp(scores - log_total[..., None]), 0.0)
    d_probs = jnp.einsum("qkgd,skd->kgqs", d_heads, value_rows, preferred_element_type=jnp.float32)
    d_scores = (probabilities * (d_probs - delta[..., None])).astype(jnp.bfloat16)
    d_query = (
        jnp.einsum("kgqs,skd->qkgd", d_scores, key_rows, preferred_element_type=jnp.float32)
        * score_scale
    )
    d_keys = (
        jnp.einsum("kgqs,qkgd->skd", d_scores, q_heads, preferred_element_type=jnp.float32)
        * score_scale
    )
    d_values = jnp.einsum(
        "kgqs,qkgd->skd",
        probabilities.astype(jnp.bfloat16),
        d_heads,
        preferred_element_type=jnp.float32,
    )
    update = jnp.concatenate(
        [d_keys.reshape(key_count, kv_width), d_values.reshape(key_count, kv_width)], axis=1
    )
    d_pairs = update
    d_query, d_pairs = (d_query, d_pairs)
    own_pairs = lax.psum_scatter(
        d_pairs.astype(jnp.bfloat16), "ctx", scatter_dimension=0, tiled=True
    ).astype(jnp.float32)
    return (d_query, own_pairs)


def forward_pass(x_block, doc_sizes, weights_now, offset):
    w_query, w_key, w_value, w_out, w_gate, w_up, w_down, gain_attn, gain_ffn = weights_now
    row_count = x_block.shape[0]
    groups = HEADS // KV_HEADS
    places = offset + jnp.arange(row_count, dtype=jnp.int32)
    segment, positions = doc_layout(doc_sizes, places)
    cosine, sine_table = rotary(positions)
    x_rows = x_block.astype(jnp.float32)
    scale_attn = rms_scale(x_rows)
    normed = (x_rows * scale_attn * gain_attn.astype(jnp.float32)).astype(jnp.bfloat16)
    queries = dot_low(normed, w_query).reshape(row_count, HEADS, HEAD)
    keys_now = dot_low(normed, w_key).reshape(row_count, KV_HEADS, HEAD)
    values_now = dot_low(normed, w_value).astype(jnp.bfloat16)
    q_heads = (
        rotate(queries, cosine, sine_table)
        .astype(jnp.bfloat16)
        .reshape(row_count, KV_HEADS, groups, HEAD)
    )
    key_flat = (
        rotate(keys_now, cosine, sine_table)
        .astype(jnp.bfloat16)
        .reshape(row_count, KV_HEADS * HEAD)
    )
    pairs = jnp.concatenate([key_flat, values_now], axis=1)
    attended, log_total = attention_forward(q_heads, pairs, doc_sizes, segment, places)
    attended_low = attended.astype(jnp.bfloat16)
    middle = x_rows + dot_low(attended_low, w_out)
    scale_ffn = rms_scale(middle)
    normed_ffn = (middle * scale_ffn * gain_ffn.astype(jnp.float32)).astype(jnp.bfloat16)
    gate_proj = dot_low(normed_ffn, w_gate)
    up_proj = dot_low(normed_ffn, w_up)
    hidden = (jax.nn.silu(gate_proj) * up_proj).astype(jnp.bfloat16)
    block_rows = (middle + dot_low(hidden, w_down)).astype(jnp.bfloat16)
    saved = (
        x_rows,
        scale_attn,
        normed,
        q_heads,
        pairs,
        segment,
        places,
        cosine,
        sine_table,
        attended,
        attended_low,
        log_total,
        middle,
        scale_ffn,
        normed_ffn,
        gate_proj,
        up_proj,
        hidden,
    )
    return (saved, block_rows)


def backward_pass(saved, back_block, doc_sizes, weights_now):
    (
        x_rows,
        scale_attn,
        normed,
        q_heads,
        pairs,
        segment,
        places,
        cosine,
        sine_table,
        attended,
        attended_low,
        log_total,
        middle,
        scale_ffn,
        normed_ffn,
        gate_proj,
        up_proj,
        hidden,
    ) = saved
    w_query, w_key, w_value, w_out, w_gate, w_up, w_down, gain_attn, gain_ffn = weights_now
    row_count = x_rows.shape[0]
    groups = HEADS // KV_HEADS
    kv_width = KV_HEADS * HEAD
    back_rows = back_block.astype(jnp.float32)
    grad_down = dot_first(hidden, back_block)
    d_hidden = dot_second(back_block, w_down)
    sigmoid_gate = jax.nn.sigmoid(gate_proj)
    d_up = (d_hidden * gate_proj * sigmoid_gate).astype(jnp.bfloat16)
    d_gate = (d_hidden * up_proj * sigmoid_gate * (1.0 + gate_proj * (1.0 - sigmoid_gate))).astype(
        jnp.bfloat16
    )
    grad_gate = dot_first(normed_ffn, d_gate)
    grad_up = dot_first(normed_ffn, d_up)
    d_normed_ffn = dot_second(d_gate, w_gate) + dot_second(d_up, w_up)
    grad_gain_ffn = jnp.sum(d_normed_ffn * middle * scale_ffn, axis=0)
    d_scaled_ffn = d_normed_ffn * gain_ffn.astype(jnp.float32)
    d_middle = (
        back_rows
        + scale_ffn * d_scaled_ffn
        - middle * scale_ffn**3 * jnp.mean(d_scaled_ffn * middle, axis=-1, keepdims=True)
    )
    d_branch = d_middle.astype(jnp.bfloat16)
    grad_out = dot_first(attended_low, d_branch)
    d_attended = dot_second(d_branch, w_out).astype(jnp.bfloat16)
    d_heads = d_attended.reshape(row_count, KV_HEADS, groups, HEAD)
    delta = jnp.sum(
        d_heads.astype(jnp.float32) * attended.reshape(row_count, KV_HEADS, groups, HEAD), axis=-1
    )
    delta = jnp.transpose(delta, (1, 2, 0))
    d_query, own_pairs = attention_backward(
        q_heads, pairs, doc_sizes, segment, places, log_total, d_heads, delta
    )
    d_query_low = (
        unrotate(d_query.reshape(row_count, HEADS, HEAD), cosine, sine_table)
        .astype(jnp.bfloat16)
        .reshape(row_count, HEADS * HEAD)
    )
    d_key_low = (
        unrotate(own_pairs[:, :kv_width].reshape(row_count, KV_HEADS, HEAD), cosine, sine_table)
        .astype(jnp.bfloat16)
        .reshape(row_count, kv_width)
    )
    d_value_low = own_pairs[:, kv_width:].astype(jnp.bfloat16)
    grad_query = dot_first(normed, d_query_low)
    grad_key = dot_first(normed, d_key_low)
    grad_value = dot_first(normed, d_value_low)
    d_normed = (
        dot_second(d_query_low, w_query)
        + dot_second(d_key_low, w_key)
        + dot_second(d_value_low, w_value)
    )
    grad_gain_attn = jnp.sum(d_normed * x_rows * scale_attn, axis=0)
    d_scaled_attn = d_normed * gain_attn.astype(jnp.float32)
    d_input = (
        d_middle
        + scale_attn * d_scaled_attn
        - x_rows * scale_attn**3 * jnp.mean(d_scaled_attn * x_rows, axis=-1, keepdims=True)
    )
    gradients = (
        grad_query,
        grad_key,
        grad_value,
        grad_out,
        grad_gate,
        grad_up,
        grad_down,
        grad_gain_attn,
        grad_gain_ffn,
    )
    return (d_input, gradients)


def body(
    tokens,
    lengths,
    gain_attn,
    w_query,
    w_key,
    w_value,
    w_out,
    gain_ffn,
    w_gate,
    w_up,
    w_down,
    cotangent,
):
    micro_count = tokens.shape[0]
    row_count = tokens.shape[1]
    ctx_count = lax.axis_size("ctx")
    offset = lax.axis_index("ctx") * row_count
    shards = (w_query, w_key, w_value, w_out, w_gate, w_up, w_down, gain_attn, gain_ffn)
    outputs = []
    input_grads = []
    summed = ()
    for micro_idx in range(micro_count):
        front = fetch_weights(shards)
        saved, block_rows = forward_pass(tokens[micro_idx], lengths[micro_idx, 0], front, offset)
        rear = fetch_weights(shards)
        d_input, gradients = backward_pass(saved, cotangent[micro_idx], lengths[micro_idx, 0], rear)
        gradients = reduce_grads(gradients, ctx_count)
        if micro_idx == 0:
            summed = gradients
        else:
            summed = tuple(
                (left_term + right_term for left_term, right_term in zip(summed, gradients))
            )
        outputs.append(block_rows)
        input_grads.append(d_input)
    return (
        jnp.stack(outputs),
        jnp.stack(input_grads),
        summed[7],
        summed[0],
        summed[1],
        summed[2],
        summed[3],
        summed[8],
        summed[4],
        summed[5],
        summed[6],
    )


def solution(mesh):
    in_specs = (
        P(None, ("dp", "ctx"), None),
        P(None, "dp", None),
        P("dp"),
        P("dp", "ctx"),
        P("dp", "ctx"),
        P("dp", "ctx"),
        P("dp", "ctx"),
        P("dp"),
        P("dp", "ctx"),
        P("dp", "ctx"),
        P("dp", "ctx"),
        P(None, ("dp", "ctx"), None),
    )
    out_specs = (
        P(None, ("dp", "ctx"), None),
        P(None, ("dp", "ctx"), None),
        P("dp"),
        P("dp", "ctx"),
        P("dp", "ctx"),
        P("dp", "ctx"),
        P("dp", "ctx"),
        P("dp"),
        P("dp", "ctx"),
        P("dp", "ctx"),
        P("dp", "ctx"),
    )
    return jax.shard_map(body, mesh=mesh, in_specs=in_specs, out_specs=out_specs, check_vma=False)
```

profile of v0, /device:TPU:1, one launch (start us, length us, event | category | flops | bytes accessed | tf_op | source)
XLA Modules:
  0.0 1793.6 jit_solution(3612026496346128795)
XLA Ops:
  7.3 19.8 %all-gather.6 = bf16[8,192,18]{1,2,0:T(8,128)(2,1)S(1)} all-gather(bf16[1,192,18]{1,2,0:T(8,128)(2,1)} %bitcast.571), channel_id=1, replica_groups=mesh['dp'=32,'ctx'=8] {'ctx'}, dimensions={0}, use_global_device_ids=true | all-gather | bytes 62208 | tf_op jit(solution)/shard_map/all_gather | solution.py:71
  28.0 14.8 all-gather.8
  43.6 14.8 all-gather.10
  60.0 14.6 all_gather.39
  74.7 71.5 %all-gather.1 = bf16[32,18,192]{2,1,0:T(8,128)(2,1)S(1)} all-gather(bf16[1,18,192]{2,1,0:T(8,128)(2,1)S(1)} %copy.70), channel_id=1, replica_groups=mesh['dp'=32,'ctx'=8] {'dp'}, dimensions={0}, use_global_device_ids=true | all-gather | bytes 228096 | tf_op jit(solution)/shard_map/all_gather | solution.py:78
  148.2 64.7 %all-reduce.39 = (bf16[576]{0:T(1024)(128)(2,1)S(1)}, bf16[576]{0:T(1024)(128)(2,1)}) all-reduce(bf16[576]{0:T(1024)(128)(2,1)S(1)} %dynamic-update-slice, bf16[576]{0:T(1024)(128)(2,1)S(1)} %dynamic-update-slice.1), channel_id=1, replica_groups=mesh['dp'=32,'ctx'=8] {'dp'}, use_global_device_ids=true, to_apply=%add | all-reduce | flops 1152 | bytes 4608
  213.1 39.8 %all_gather.37 = bf16[18,192]{0,1:T(8,128)(2,1)S(1)} all-gather(bf16[18,24]{0,1:T(8,128)(2,1)S(1)} %copy.66), channel_id=1, replica_groups=mesh['dp'=32,'ctx'=8] {'ctx'}, dimensions={1}, use_global_device_ids=true | all-gather | bytes 7776 | tf_op jit(solution)/shard_map/all_gather | solution.py:68
  252.9 67.1 %all-gather = bf16[32,18,192]{2,1,0:T(8,128)(2,1)S(1)} all-gather(bf16[1,18,192]{2,1,0:T(8,128)(2,1)S(1)} %copy.67), channel_id=1, replica_groups=mesh['dp'=32,'ctx'=8] {'dp'}, dimensions={0}, use_global_device_ids=true | all-gather | bytes 228096 | tf_op jit(solution)/shard_map/all_gather | solution.py:77
  322.9 27.4 %all-gather.2 = bf16[8,72,18]{1,2,0:T(8,128)(2,1)S(1)} all-gather(bf16[1,72,18]{1,2,0:T(8,128)(2,1)S(1)} %bitcast.576), channel_id=1, replica_groups=mesh['dp'=32,'ctx'=8] {'ctx'}, dimensions={0}, use_global_device_ids=true | all-gather | bytes 23328 | tf_op jit(solution)/shard_map/all_gather | solution.py:67
  350.5 70.0 %all-gather.3 = bf16[32,18,576]{2,1,0:T(8,128)(2,1)S(1)} all-gather(bf16[1,18,576]{2,1,0:T(8,128)(2,1)S(1)} %bitcast.563), channel_id=1, replica_groups=mesh['dp'=32,'ctx'=8] {'dp'}, dimensions={0}, use_global_device_ids=true | all-gather | bytes 684288 | tf_op jit(solution)/shard_map/all_gather | solution.py:76
  424.7 32.7 %all_gather.53 = bf16[1024,384]{0,1:T(8,128)(2,1)S(1)} all-gather(bf16[128,384]{0,1:T(8,128)(2,1)S(1)} %pad_maximum_fusion.7), channel_id=1, replica_groups=mesh['dp'=32,'ctx'=8] {'ctx'}, dimensions={0}, use_global_device_ids=true | all-gather | bytes 884736 | tf_op jit(solution)/shard_map/all_gather | solution.py:176
  459.0 14.6 all-gather.4
  473.7 68.1 %all-gather.5 = bf16[32,18,576]{2,1,0:T(8,128)(2,1)S(1)} all-gather(bf16[1,18,576]{2,1,0:T(8,128)(2,1)S(1)} %bitcast.564), channel_id=1, replica_groups=mesh['dp'=32,'ctx'=8] {'dp'}, dimensions={0}, use_global_device_ids=true | all-gather | bytes 684288 | tf_op jit(solution)/shard_map/all_gather | solution.py:79
  543.8 31.7 %all_gather.41 = bf16[1024,384]{0,1:T(8,128)(2,1)S(1)} all-gather(bf16[128,384]{0,1:T(8,128)(2,1)S(1)} %pad_maximum_fusion.6), channel_id=1, replica_groups=mesh['dp'=32,'ctx'=8] {'ctx'}, dimensions={0}, use_global_device_ids=true | all-gather | bytes 884736 | tf_op jit(solution)/shard_map/all_gather | solution.py:176
  592.5 2.8 reshape.542
  595.3 2.6 reshape.546
  601.7 3.7 multiply_convert_fusion.2
  621.4 3.6 fusion.46
  643.6 9.8 reduce-scatter.51.cloned.1.call-done
  654.4 38.2 %reduce-scatter.53.cloned.1.call-done = bf16[128,384]{1,0:T(8,128)(2,1)} async-done(((bf16[1024,384]{1,0:T(8,128)(2,1)}), bf16[128,384]{1,0:T(8,128)(2,1)}) %reduce-scatter.53.cloned.1.call-update) | async-done | bytes 98320
  697.1 126.2 %fusion.174 = (bf16[24,192]{1,0:T(8,128)(2,1)}, bf16[24,192]{1,0:T(8,128)(2,1)}, bf16[24,192]{1,0:T(8,128)(2,1)}, bf16[24,192]{1,0:T(8,128)(2,1)S(1)}, bf16[24,1...) fusion(bf16[576,192]{1,0:T(8,128)(2,1)S(1)} %convolution_convert_fusio, ...), kind=kCustom, calls=%all-reduce-scatter.8 | all-reduce-scatter fusion | flops 5308417 | bytes 8295424
  827.2 5.6 collective-permute-start.39
  836.4 3.7 collective-permute-start.45
  844.3 3.1 collective-permute-start.63
  848.8 3.0 collective-permute-start.42
  856.3 7.5 collective-permute-start.38
  863.8 3.7 collective-permute-start.37
  869.6 3.1 collective-permute-start.35
  872.8 3.7 collective-permute-start.34
  890.8 3.4 collective-permute-start.58
  901.4 2.6 collective-permute-start.54
  912.8 4.0 collective-permute-start.50
  939.9 4.0 collective-permute-start.14
  951.2 2.9 collective-permute-start.7
  956.6 65.2 %all-reduce.38 = (bf16[576]{0:T(1024)(128)(2,1)S(1)}, bf16[576]{0:T(1024)(128)(2,1)S(1)}, bf16[576]{0:T(1024)(128)(2,1)S(1)}, bf16[576]{0:T(1024)(128)(2,1)S(1)}) all-reduce(bf16[576]{0:T(1024)(128)(2,1)S(1)} %copy-done.98, bf16[576]{0:T(1024)(128)(2,1)S(1)} %get-tuple-element.15, ...), channel_id=8, replica_groups=mesh['dp'=32,'ctx'=8] {'dp'}, use_global_device_ids=true, to_apply=%region_32.33.clone | all-reduce | flops 2304 | bytes 9216
  1023.1 3.9 collective-permute-start.23
  1029.7 5.0 collective-permute-start.9
  1036.1 7.5 collective-permute-start.6
  1045.9 3.7 collective-permute-start.4
  1051.8 5.1 collective-permute-start.2
  1058.4 3.1 collective-permute-start
  1069.6 3.7 collective-permute-start.26
  1077.8 2.8 collective-permute-start.22
  1085.2 3.7 collective-permute-start.18
  1104.6 243.2 %all-reduce.46.cloned.1.call-done = (bf16[576,576]{1,0:T(8,128)(2,1)}, bf16[576,576]{1,0:T(8,128)(2,1)}, bf16[576,576]{1,0:T(8,128)(2,1)}, bf16[576,576]{1,0:T(8,128)(2,1)}) async-done(((bf16[576,576]{1,0:T(8,128)(2,1)}, bf16[576,576]{1,0:T(8,128)(2,1)}, bf16[576,576]{1,0:T(8,128)(2,1)}, bf16[576,576]{1,0:T(8,128)(2,1)}), (bf16[576,576]{1,0:T(8,128)(2,1)}, bf16[576,576]{1,0:T(8,128)(2,1)}, ...) | async-done | bytes 2654224
  1353.3 159.4 %reduce-scatter.49.cloned.1.call-done = bf16[48,576]{1,0:T(8,128)(2,1)} async-done(((bf16[1536,576]{1,0:T(8,128)(2,1)}), bf16[48,576]{1,0:T(8,128)(2,1)}) %reduce-scatter.49.cloned.1.call-update) | async-done | bytes 55312 | tf_op jit(solution)/shard_map/reduce_scatter | solution.py:108
  1512.7 164.6 %reduce-scatter.47.cloned.1.call-done = bf16[48,576]{1,0:T(8,128)(2,1)} async-done(((bf16[1536,576]{1,0:T(8,128)(2,1)}), bf16[48,576]{1,0:T(8,128)(2,1)}) %reduce-scatter.47.cloned.1.call-update) | async-done | bytes 55312 | tf_op jit(solution)/shard_map/reduce_scatter | solution.py:108
  1679.2 97.3 %all-reduce.48.cloned.1.call-done = (bf16[8,2,18]{2,1,0:T(2,128)(2,1)}, bf16[8,2,18]{2,1,0:T(2,128)(2,1)}, bf16[18,576]{1,0:T(8,128)(2,1)}, bf16[18,576]{1,0:T(8...) async-done(((bf16[8,2,18]{2,1,0:T(2,128)(2,1)}, ...) | async-done | bytes 222352
  (596 shorter events, 215.8 us)
Async XLA Ops:
  7.2 585.2 %all-gather.17.cloned.1.call-start = ((), (), s32[]{:S(2)}) async-start(), calls=%async_computation.11 | async-start | bytes 2433024 | tf_op jit(solution)/shard_map/all_gather | solution.py:80
  27.9 567.3 %all-gather.19.cloned.1.call-start = ((), (), s32[]{:S(2)}) async-start(), calls=%async_computation.12 | async-start | bytes 2433024 | tf_op jit(solution)/shard_map/all_gather | solution.py:81
  43.5 558.2 %all-gather.15.cloned.1.call-start = ((), (), s32[]{:S(2)}) async-start(), calls=%async_computation.8 | async-start | bytes 2027520 | tf_op jit(solution)/shard_map/all_gather | solution.py:82
  59.2 594.2 %reduce-scatter.51.cloned.1.call-start = ((), (), s32[]{:S(2)}) async-start(), calls=%async_computation.13 | async-start | bytes 884736
  620.7 71.9 %reduce-scatter.53.cloned.1.call-start = ((), (), s32[]{:S(2)}) async-start(), calls=%async_computation.14 | async-start | bytes 884736
  635.4 464.9 %reduce-scatter.57.cloned.1.call-start = ((), (), s32[]{:S(2)}) async-start(), calls=%async_computation.16 | async-start | bytes 442368
  824.3 18.0 %collective-permute-start.47 = (bf16[18,1536]{1,0:T(8,128)(2,1)S(1)}, bf16[18,1536]{1,0:T(8,128)(2,1)S(1)}, u32[]{:S(2)}, u32[]{:S(2)}) collective-permute-start(bf16[18,1536]{1,0:T(8,128)(2,1)S(1)} %slice.181), channel_id=1, source_target_pairs={{0,64},{8,72},{16,80},{24,88},{32,96},{40,104},{48,112},{56,120},{... | collective-permute-start | bytes 165896
  827.2 17.0 collective-permute-start.39
  835.1 16.8 collective-permute-start.46
  836.4 17.8 collective-permute-start.45
  840.1 16.2 collective-permute-start.44
  842.3 21.5 %collective-permute-start.43 = (bf16[24,1536]{1,0:T(8,128)(2,1)}, bf16[24,1536]{1,0:T(8,128)(2,1)S(1)}, u32[]{:S(2)}, u32[]{:S(2)}) collective-permute-start(bf16[24,1536]{1,0:T(8,128)(2,1)} %get-tuple-element.63), channel_id=1, source_target_pairs={{0,32},{8,40},{16,48},{24,56},{32,64},{40,72},{48,80},{56,88},{64,... | collective-permute-start | bytes 221192
  848.8 19.5 %collective-permute-start.42 = (bf16[24,1536]{1,0:T(8,128)(2,1)}, bf16[24,1536]{1,0:T(8,128)(2,1)S(1)}, u32[]{:S(2)}, u32[]{:S(2)}) collective-permute-start(bf16[24,1536]{1,0:T(8,128)(2,1)} %get-tuple-element.63), channel_id=1, source_target_pairs={{0,24},{8,32},{16,40},{24,48},{32,56},{40,64},{48,72},{56,80},{64,... | collective-permute-start | bytes 221192
  851.9 17.8 collective-permute-start.41
  854.1 18.6 %collective-permute-start.40 = (bf16[24,1536]{1,0:T(8,128)(2,1)}, bf16[24,1536]{1,0:T(8,128)(2,1)S(1)}, u32[]{:S(2)}, u32[]{:S(2)}) collective-permute-start(bf16[24,1536]{1,0:T(8,128)(2,1)} %get-tuple-element.63), channel_id=1, source_target_pairs={{0,8},{8,16},{16,24},{24,32},{32,40},{40,48},{48,56},{56,64},{64,7... | collective-permute-start | bytes 221192
  856.3 20.2 %collective-permute-start.38 = (bf16[24,1536]{1,0:T(8,128)(2,1)}, bf16[24,1536]{1,0:T(8,128)(2,1)S(1)}, u32[]{:S(2)}, u32[]{:S(2)}) collective-permute-start(bf16[24,1536]{1,0:T(8,128)(2,1)} %get-tuple-element.64), channel_id=1, source_target_pairs={{0,56},{8,64},{16,72},{24,80},{32,88},{40,96},{48,104},{56,112},{6... | collective-permute-start | bytes 221192
  863.8 14.6 collective-permute-start.37
  868.3 15.0 collective-permute-start.36
  869.6 16.3 collective-permute-start.35
  872.8 14.7 collective-permute-start.34
  887.5 13.9 collective-permute-start.60
  889.2 14.9 collective-permute-start.59
  890.8 15.2 collective-permute-start.58
  895.2 206.1 %reduce-scatter.55.cloned.1.call-start = ((), (), s32[]{:S(2)}) async-start(), calls=%async_computation.15 | async-start | bytes 442368
  901.4 15.4 collective-permute-start.54
  904.1 14.7 collective-permute-start.53
  908.3 193.8 %reduce-scatter.61.cloned.1.call-start = ((), (), s32[]{:S(2)}) async-start(), calls=%async_computation.18 | async-start | bytes 442368
  908.4 14.0 collective-permute-start.52
  922.4 180.7 %reduce-scatter.59.cloned.1.call-start = ((), (), s32[]{:S(2)}) async-start(), calls=%async_computation.17 | async-start | bytes 442368
  925.3 422.5 %all-reduce.46.cloned.1.call-start = ((), (), s32[]{:S(2)}) async-start(), calls=%async_computation.19 | async-start | bytes 5898240
  926.6 586.1 %reduce-scatter.49.cloned.1.call-start = ((), (), s32[]{:S(2)}) async-start(), calls=%async_computation.10 | async-start | bytes 2027520 | tf_op jit(solution)/shard_map/reduce_scatter | solution.py:108
  928.7 748.7 %reduce-scatter.47.cloned.1.call-start = ((), (), s32[]{:S(2)}) async-start(), calls=%async_computation.9 | async-start | bytes 2027520 | tf_op jit(solution)/shard_map/reduce_scatter | solution.py:108
  939.8 836.7 %all-reduce.48.cloned.1.call-start = ((), (), s32[]{:S(2)}) async-start(), calls=%async_computation.20 | async-start | bytes 606208
  939.9 89.8 %collective-permute-start.14 = (bf16[24,192]{1,0:T(8,128)(2,1)S(1)}, bf16[24,192]{1,0:T(8,128)(2,1)S(1)}, u32[]{:S(2)}, u32[]{:S(2)}) collective-permute-start(bf16[24,192]{1,0:T(8,128)(2,1)S(1)} %copy-done.89), channel_id=1, source_target_pairs={{0,56},{8,64},{16,72},{24,80},{32,88},{40,96},{48,104},{56,112},{6... | collective-permute-start | bytes 27656
  943.9 90.8 %collective-permute-start.13 = (bf16[24,192]{1,0:T(8,128)(2,1)S(1)}, bf16[24,192]{1,0:T(8,128)(2,1)S(1)}, u32[]{:S(2)}, u32[]{:S(2)}) collective-permute-start(bf16[24,192]{1,0:T(8,128)(2,1)S(1)} %copy-done.89), channel_id=1, source_target_pairs={{0,48},{8,56},{16,64},{24,72},{32,80},{40,88},{48,96},{56,104},{64... | collective-permute-start | bytes 27656
  946.4 89.6 %collective-permute-start.12 = (bf16[24,192]{1,0:T(8,128)(2,1)S(1)}, bf16[24,192]{1,0:T(8,128)(2,1)S(1)}, u32[]{:S(2)}, u32[]{:S(2)}) collective-permute-start(bf16[24,192]{1,0:T(8,128)(2,1)S(1)} %copy-done.89), channel_id=1, source_target_pairs={{0,40},{8,48},{16,56},{24,64},{32,72},{40,80},{48,88},{56,96},{64,... | collective-permute-start | bytes 27656
  949.0 72.7 %collective-permute-start.15 = (bf16[18,192]{1,0:T(8,128)(2,1)S(1)}, bf16[18,192]{1,0:T(8,128)(2,1)S(1)}, u32[]{:S(2)}, u32[]{:S(2)}) collective-permute-start(bf16[18,192]{1,0:T(8,128)(2,1)S(1)} %slice.177), channel_id=1, source_target_pairs={{0,64},{8,72},{16,80},{24,88},{32,96},{40,104},{48,112},{56,120},{... | collective-permute-start | bytes 20744
  951.2 71.9 %collective-permute-start.7 = (bf16[18,192]{1,0:T(8,128)(2,1)S(1)}, bf16[18,192]{1,0:T(8,128)(2,1)S(1)}, u32[]{:S(2)}, u32[]{:S(2)}) collective-permute-start(bf16[18,192]{1,0:T(8,128)(2,1)S(1)} %slice.176), channel_id=1, source_target_pairs={{0,64},{8,72},{16,80},{24,88},{32,96},{40,104},{48,112},{56,120},{... | collective-permute-start | bytes 20744
  1027.1 16.5 collective-permute-start.11
  1028.4 17.5 collective-permute-start.10
  1029.7 19.9 %collective-permute-start.9 = (bf16[24,192]{1,0:T(8,128)(2,1)S(1)}, bf16[24,192]{1,0:T(8,128)(2,1)S(1)}, u32[]{:S(2)}, u32[]{:S(2)}) collective-permute-start(bf16[24,192]{1,0:T(8,128)(2,1)S(1)} %copy-done.89), channel_id=1, source_target_pairs={{0,16},{8,24},{16,32},{24,40},{32,48},{40,56},{48,64},{56,72},{64,... | collective-permute-start | bytes 27656
  1034.8 17.1 collective-permute-start.8
  1036.1 20.9 %collective-permute-start.6 = (bf16[24,192]{1,0:T(8,128)(2,1)S(1)}, bf16[24,192]{1,0:T(8,128)(2,1)S(1)}, u32[]{:S(2)}, u32[]{:S(2)}) collective-permute-start(bf16[24,192]{1,0:T(8,128)(2,1)S(1)} %copy-done.88), channel_id=1, source_target_pairs={{0,56},{8,64},{16,72},{24,80},{32,88},{40,96},{48,104},{56,112},{6... | collective-permute-start | bytes 27656
  1043.6 14.8 collective-permute-start.5
  1045.9 15.6 collective-permute-start.4
  1049.7 14.4 collective-permute-start.3
  1051.8 14.4 collective-permute-start.2
  1081.9 14.8 collective-permute-start.20
  (154 other events, 4194.5 us)
Sparse Core Ops, SparseCore 0:
  28.0 134.7 all-gather.16
  164.6 157.3 all-gather.18
  323.8 157.1 all-gather.14
  620.8 32.5 reduce-scatter.50
  655.9 36.6 reduce-scatter.52
  895.3 36.4 reduce-scatter.56
  934.5 35.2 reduce-scatter.54
  972.3 35.3 reduce-scatter.60
  1010.4 35.1 reduce-scatter.58
  1048.4 299.3 all-reduce.45
  1350.4 162.2 reduce-scatter.48
  1515.1 162.2 reduce-scatter.46
  1682.7 93.8 all-reduce.47
where the time goes:
time: 1800 us; the launch traced here: 1790 us
  blocking collectives  743 us (41%)
  waiting for transfers between devices  715 us (40%)
  starting transfers between devices  168 us (9%)
  matrix products  61.1 us (3%)
  local copies, waits for them, and re-layouts  55.7 us (3%)
  other arithmetic  30.3 us (2%)
  between operations  20.6 us (1%)
    unnamed x85, waiting for transfers between devices  391 us
    reduce_scatter x2, waiting for transfers between devices, reduce_grads(): lax.psum_scatter(gradients[6].astype(jnp.bfloat16), 'dp', scatter_dimensi...  324 us
    unnamed x3, blocking collectives  256 us
    unnamed x72, starting transfers between devices  168 us
    all_gather x1, blocking collectives, fetch_weights(): lax.all_gather(widened[2], 'dp', axis=0, tiled=True)  71.5 us
    all_gather x1, blocking collectives, fetch_weights(): lax.all_gather(widened[0], 'dp', axis=0, tiled=True)  70 us
    all_gather x1, blocking collectives, fetch_weights(): lax.all_gather(widened[3], 'dp', axis=0, tiled=True)  68.1 us
    all_gather x1, blocking collectives, fetch_weights(): lax.all_gather(widened[1], 'dp', axis=0, tiled=True)  67.1 us
  transfers between devices with their start and end apart: 77, of which 8 were waited for; matrix products, arithmetic and copies ran while one was open for 6% of the time, Pallas kernels for 0%

commit v1 on v0

v1 whole, which is shorter than its diff:
```python
import jax
import jax.numpy as jnp
from jax import lax
from jax.experimental import pallas as pl
from jax.experimental.pallas import tpu as pltpu
from jax.sharding import Mesh
from jax.sharding import PartitionSpec as P

HEADS = 9
KV_HEADS = 3
HEAD = 64
D = 576
FF = 1536
GROUP = 1024
STRETCH = 128
LANES = 128
CHUNK = 256
FF_CHUNK = 512
PAD_K = 640
BLOCK_K = 40
EPSILON = 1e-05
ROPE_BASE = 100000.0
MASKED = -1e30
F32 = jnp.float32
BF16 = jnp.bfloat16


def mm(a, b):
    return lax.dot_general(a, b, (((1,), (0,)), ((), ())), preferred_element_type=F32)


def mm_nt(a, b):
    return lax.dot_general(a, b, (((1,), (1,)), ((), ())), preferred_element_type=F32)


def mm_tn(a, b):
    return lax.dot_general(a, b, (((0,), (0,)), ((), ())), preferred_element_type=F32)


def rotate_lanes(values, cosine, sine_low, sine_high):
    parts = []
    for start in range(0, values.shape[1], LANES):
        part = values[:, start : start + LANES]
        parts.append(
            part * cosine
            + pltpu.roll(part, LANES - HEAD // 2, 1) * sine_low
            + pltpu.roll(part, HEAD // 2, 1) * sine_high
        )
    return jnp.concatenate(parts, axis=1)


def unpermute(values, table):
    high = values.astype(BF16)
    low = (values - high.astype(F32)).astype(BF16)
    return mm_nt(high, table) + mm_nt(low, table)


def inverse_rms(values):
    return lax.rsqrt(jnp.mean(values * values, axis=-1, keepdims=True) + EPSILON)


def own_rows(ref):
    return jnp.concatenate([ref[pl.ds(0, STRETCH), :], ref[pl.ds(GROUP, STRETCH), :]], axis=0)


def layer_kernel(
    x_ref,
    back_ref,
    bias_ref,
    cos_ref,
    low_ref,
    high_ref,
    place_a_ref,
    place_b_ref,
    place_bt_ref,
    rows_ref,
    lanes_ref,
    attn_w_ref,
    gate_w_ref,
    up_w_ref,
    down_w_ref,
    core_ref,
    *refs,
):
    out_ref, d_middle_ref, d_normed_ref, d_pairs_ref, w_pairs_ref, gain_ref = refs[:6]
    mine_a, other_a, mine_t, other_t, mine_d, other_d = (
        refs[6 + 4 * i : 10 + 4 * i] for i in range(6)
    )
    (
        attn_w,
        normed,
        keys,
        values,
        probs,
        mixed,
        mixed_low,
        middle_ref,
        hidden_ref,
        d_gate_s,
        d_up_s,
        d_query,
        shared,
        attn_g,
    ) = refs[30:]
    core, x_pos, y_pos = core_ref[0], core_ref[1], core_ref[2]

    def put(first, second, cols, value):
        @pl.when(core == 0)
        def _():
            for k in range(4):
                first[k][:, cols] = value[k * 160 : (k + 1) * 160]

        @pl.when(core == 1)
        def _():
            for k in range(4):
                second[k][:, cols] = value[k * 160 : (k + 1) * 160]

    groups = HEADS // KV_HEADS
    own = 2 * STRETCH
    chunks = 2 * GROUP // CHUNK
    gain_rows = attn_w_ref[:, :LANES]
    row_mask = rows_ref[...].astype(F32)
    gain_attn = jnp.sum(mm(gain_rows, lanes_ref[0]) * row_mask, axis=0, keepdims=True)
    gain_ffn = jnp.sum(mm(gain_rows, lanes_ref[1]) * row_mask, axis=0, keepdims=True)
    gain_ref[...] = gain_attn
    for start in range(0, FF, FF_CHUNK):
        cols = slice(start, start + FF_CHUNK)
        attn_w[:, cols] = mm(place_b_ref[...], attn_w_ref[:, cols]).astype(BF16)
    w_pairs_ref[:, :256] = attn_w[:, 512:768]
    w_pairs_ref[:, 256:] = attn_w[:, 1280:]

    def project(step, carry):
        rows = pl.ds(pl.multiple_of(step * CHUNK, CHUNK), CHUNK)
        x_rows = x_ref[rows, :].astype(F32)
        scaled = (x_rows * inverse_rms(x_rows) * gain_attn).astype(BF16)
        normed[rows, :] = scaled
        turned_keys = rotate_lanes(
            mm(scaled, attn_w[:, 512:768]), cos_ref[rows, :], low_ref[rows, :], high_ref[rows, :]
        )
        keys[rows, :] = turned_keys.astype(BF16)
        values[rows, :] = mm(scaled, attn_w[:, 1280:]).astype(BF16)
        return carry

    lax.fori_loop(0, chunks, project, 0)

    cos_own, low_own, high_own = own_rows(cos_ref), own_rows(low_ref), own_rows(high_ref)
    normed_own = own_rows(normed)
    scale = HEAD ** (-0.5)
    queries = rotate_lanes(mm(normed_own, attn_w[:, :640]), cos_own, low_own, high_own)
    queries = (queries.astype(BF16).astype(F32) * scale).astype(BF16)

    def stacked(array, micro, group):
        rows = slice(micro * STRETCH, (micro + 1) * STRETCH)
        return jnp.concatenate(
            [
                array[rows, HEAD * (group * groups + j) : HEAD * (1 + group * groups + j)]
                for j in range(groups)
            ],
            axis=0,
        )

    for micro in range(2):
        bias = bias_ref[micro]
        bias = jnp.concatenate([bias] * groups, axis=0)
        rows = slice(micro * GROUP, (micro + 1) * GROUP)
        for group in range(KV_HEADS):
            key_rows = keys[rows, HEAD * (group + 1) : HEAD * (group + 2)]
            value_rows = values[rows, HEAD * (group + 1) : HEAD * (group + 2)]
            scores = mm_nt(stacked(queries, micro, group), key_rows) + bias
            weights = jnp.exp(scores - jnp.max(scores, axis=-1, keepdims=True))
            total = jnp.sum(weights, axis=-1, keepdims=True)
            low_probs = (weights * (1.0 / total)).astype(BF16)
            probs[micro * KV_HEADS + group] = low_probs
            mix = mm(low_probs, value_rows)
            mixed[micro * KV_HEADS + group] = mix
            for j in range(groups):
                head = group * groups + j
                mixed_low[
                    micro * STRETCH : (micro + 1) * STRETCH, HEAD * head : HEAD * (head + 1)
                ] = mix[j * STRETCH : (j + 1) * STRETCH].astype(BF16)

    x_own = own_rows(x_ref).astype(F32)
    middle = x_own + mm(mixed_low[...], attn_w[:, 768:1344])
    middle_ref[...] = middle
    scale_ffn = inverse_rms(middle)
    normed_ffn = mm((middle * scale_ffn * gain_ffn).astype(BF16), place_a_ref[...]).astype(BF16)
    back = back_ref[...]
    for start in range(0, FF, FF_CHUNK):
        cols = slice(start, start + FF_CHUNK)
        gate = mm(normed_ffn, gate_w_ref[:, cols])
        up = mm(normed_ffn, up_w_ref[:, cols])
        sig = 1.0 / (1.0 + jnp.exp(-gate))
        silu = gate * sig
        hidden_ref[:, cols] = (silu * up).astype(BF16)
        d_hidden = mm_nt(back, down_w_ref[cols, :])
        d_gate_s[:, cols] = (d_hidden * up * (sig + silu * (1.0 - sig))).astype(BF16)
        d_up_s[:, cols] = (d_hidden * silu).astype(BF16)
    hidden = hidden_ref[...]
    out_ref[...] = (middle + mm(hidden, down_w_ref[...])).astype(BF16)
    d_rows = jnp.zeros((2 * STRETCH, PAD_K), F32)
    for start in range(0, FF, FF_CHUNK):
        cols = slice(start, start + FF_CHUNK)
        d_gate, d_up = d_gate_s[:, cols], d_up_s[:, cols]
        shared[cols, :D] = mm_tn(hidden_ref[:, cols], back)
        put(mine_a, other_a, cols, mm_tn(normed_ffn, d_gate).astype(BF16))
        put(other_a, mine_a, cols, mm_tn(normed_ffn, d_up).astype(BF16))
        d_rows = d_rows + mm_nt(d_gate, gate_w_ref[:, cols]) + mm_nt(d_up, up_w_ref[:, cols])
    d_normed_ffn = unpermute(d_rows, place_a_ref[...])
    middle = middle_ref[...]
    g_gain_ffn = jnp.sum(d_normed_ffn * middle * scale_ffn, axis=0, keepdims=True)
    d_scaled = d_normed_ffn * gain_ffn
    d_middle = (
        back.astype(F32)
        + scale_ffn * d_scaled
        - middle * scale_ffn**3 * jnp.mean(d_scaled * middle, axis=-1, keepdims=True)
    )
    d_middle_ref[...] = d_middle
    d_branch = d_middle.astype(BF16)
    attn_g[:, 768:1344] = mm_tn(mixed_low[...], d_branch).astype(BF16)
    d_mixed = mm_nt(d_branch, attn_w[:, 768:1344]).astype(BF16)

    def split_down(first_part, second_part):
        for k in range(4):
            y_index = lax.rem(y_pos + 4 - k, 4)
            for j in range(4):
                x_index = lax.rem(x_pos + 4 - j, 4)
                for z in range(2):
                    start = (z * 16 + x_index * 4 + y_index) * 48
                    for half, part in enumerate((first_part, second_part)):
                        rows = pl.ds(pl.multiple_of(start + half * 24, 8), 24)
                        part[k][2 * j + z] = shared[rows, :D].astype(BF16)

    @pl.when(core == 0)
    def _():
        split_down(mine_d, other_d)

    @pl.when(core == 1)
    def _():
        split_down(other_d, mine_d)

    d_query[...] = jnp.zeros_like(d_query)
    shared[...] = jnp.zeros_like(shared)
    for micro in range(2):
        rows = slice(micro * GROUP, (micro + 1) * GROUP)
        own_part = slice(micro * STRETCH, (micro + 1) * STRETCH)
        for group in range(KV_HEADS):
            key_rows = keys[rows, HEAD * (group + 1) : HEAD * (group + 2)]
            value_rows = values[rows, HEAD * (group + 1) : HEAD * (group + 2)]
            d_mix = jnp.concatenate(
                [
                    d_mixed[
                        own_part, HEAD * (group * groups + j) : HEAD * (group * groups + j + 1)
                    ]
                    for j in range(groups)
                ],
                axis=0,
            )
            delta = jnp.sum(
                d_mix.astype(F32) * mixed[micro * KV_HEADS + group], axis=-1, keepdims=True
            )
            low_probs = probs[micro * KV_HEADS + group]
            d_probs = mm_nt(d_mix, value_rows)
            d_scores = (low_probs.astype(F32) * (d_probs - delta)).astype(BF16)
            d_rows = mm(d_scores, key_rows) * scale
            for j in range(groups):
                head = group * groups + j
                d_query[own_part, HEAD * head : HEAD * (head + 1)] = d_rows[
                    j * STRETCH : (j + 1) * STRETCH
                ]
            shared[rows, HEAD * (group + 1) : HEAD * (group + 2)] = mm_tn(
                d_scores, stacked(queries, micro, group)
            )
            shared[rows, 256 + HEAD * (group + 1) : 256 + HEAD * (group + 2)] = mm_tn(
                low_probs, d_mix
            )

    d_query_low = rotate_lanes(d_query[...], cos_own, -low_own, -high_own).astype(BF16)
    g_query = mm_tn(normed_own, d_query_low)
    d_normed = mm_nt(d_query_low, attn_w[:, :640])
    d_normed_ref[...] = d_normed
    g_gain_attn = jnp.sum(d_normed * x_own * inverse_rms(x_own), axis=0, keepdims=True)

    def finish(step, carry):
        rows = pl.ds(pl.multiple_of(step * CHUNK, CHUNK), CHUNK)
        key_part = rotate_lanes(
            shared[rows, :256], cos_ref[rows, :], -low_ref[rows, :], -high_ref[rows, :]
        ).astype(BF16)
        value_part = shared[rows, 256:512].astype(BF16)
        d_pairs_ref[rows, :256] = key_part
        d_pairs_ref[rows, 256:] = value_part
        x_rows = x_ref[rows, :].astype(F32)
        d_rows = mm_nt(key_part, attn_w[:, 512:768]) + mm_nt(value_part, attn_w[:, 1280:])
        return carry + jnp.sum(d_rows * x_rows * inverse_rms(x_rows), axis=0, keepdims=True)

    g_gain_attn = lax.fori_loop(0, chunks, finish, g_gain_attn)
    gain_block = mm_nt(row_mask.astype(BF16) * g_gain_attn.astype(BF16), lanes_ref[0])
    gain_block = gain_block + mm_nt(row_mask.astype(BF16) * g_gain_ffn.astype(BF16), lanes_ref[1])
    all_normed = normed[...]
    g_key = mm_tn(all_normed, d_pairs_ref[:, :256])
    g_value = mm_tn(all_normed, d_pairs_ref[:, 256:])
    attn_g[:, :576] = g_query[:, :576].astype(BF16)
    attn_g[:, 576:768] = g_key[:, 64:].astype(BF16)
    attn_g[:, 1344:1536] = g_value[:, 64:].astype(BF16)
    for start in (0, 768):
        part = mm(place_bt_ref[...], attn_g[:, start : start + 768])
        first, second = (mine_t, other_t) if start == 0 else (other_t, mine_t)
        put(first, second, slice(LANES, 768), part[:, LANES:].astype(BF16))
        put(first, second, slice(0, LANES), (part[:, :LANES] + gain_block).astype(BF16))


def assemble_kernel(core_ref, *refs):
    mine_a, other_a, mine_t, other_t, mine_d, other_d = (
        refs[4 * i : 4 + 4 * i] for i in range(6)
    )
    gate_ref, up_ref, attn_ref, down_ref = refs[24:]
    core, x_pos, y_pos = core_ref[0], core_ref[1], core_ref[2]

    def join(gate_part, up_part, query_part, out_part, first_part, second_part):
        for k in range(4):
            rows = slice(k * 160, (k + 1) * 160)
            gate_ref[rows, :] = gate_part[k][...]
            up_ref[rows, :] = up_part[k][...]
            attn_ref[rows, :768] = query_part[k][...]
            attn_ref[rows, 768:] = out_part[k][...]
            y_index = lax.rem(y_pos + 4 - k, 4)
            for j in range(4):
                x_index = lax.rem(x_pos + 4 - j, 4)
                for z in range(2):
                    for half, part in enumerate((first_part, second_part)):
                        down_ref[z * 16 + x_index * 4 + y_index, half] = part[k][2 * j + z]

    @pl.when(core == 0)
    def _():
        join(mine_a, other_a, mine_t, other_t, mine_d, other_d)

    @pl.when(core == 1)
    def _():
        join(other_a, mine_a, other_t, mine_t, other_d, mine_d)


def final_kernel(
    x_ref, gain_ref, w_pairs_ref, d_middle_ref, d_normed_ref, *refs
):
    piece_refs, out_ref = refs[:-1], refs[-1]
    d_pairs = piece_refs[0][...].astype(F32)
    for piece in piece_refs[1:]:
        d_pairs = d_pairs + piece[...].astype(F32)
    d_pairs = d_pairs.astype(BF16)
    x_rows = x_ref[...].astype(F32)
    scale = inverse_rms(x_rows)
    d_scaled = (d_normed_ref[...] + mm_nt(d_pairs, w_pairs_ref[...])) * gain_ref[...]
    out_ref[...] = (
        d_middle_ref[...]
        + scale * d_scaled
        - x_rows * scale**3 * jnp.mean(d_scaled * x_rows, axis=-1, keepdims=True)
    )


def vmem_call(kernel, outs, scratch=(), flops=0, moved=0, specs=None):
    return pl.pallas_call(
        kernel,
        out_shape=outs,
        **({} if specs is None else {"in_specs": specs}),
        scratch_shapes=list(scratch),
        compiler_params=pltpu.CompilerParams(vmem_limit_bytes=60 * 1024 * 1024),
        cost_estimate=pl.CostEstimate(flops=flops, bytes_accessed=moved, transcendentals=0),
    )


def run_layer(x_all, back, tables, places, gain_maps, weights, spot):
    own = 2 * STRETCH
    full = 2 * GROUP
    shape = jax.ShapeDtypeStruct
    outs = (
        shape((own, D), BF16),
        shape((own, D), F32),
        shape((own, D), F32),
        shape((full, 512), BF16),
        shape((D, 512), BF16),
        shape((1, D), F32),
    )
    outs = outs + (shape((160, FF), BF16),) * 8
    outs = outs + (shape((160, 768), BF16),) * 8
    outs = outs + (shape((8, 24, D), BF16),) * 8
    scratch = (
        pltpu.VMEM((D, FF), BF16),
        pltpu.VMEM((full, D), BF16),
        pltpu.VMEM((full, 256), BF16),
        pltpu.VMEM((full, 256), BF16),
        pltpu.VMEM((6, 3 * STRETCH, GROUP), BF16),
        pltpu.VMEM((6, 3 * STRETCH, HEAD), F32),
        pltpu.VMEM((own, D), BF16),
        pltpu.VMEM((own, D), F32),
        pltpu.VMEM((own, FF), BF16),
        pltpu.VMEM((own, FF), BF16),
        pltpu.VMEM((own, FF), BF16),
        pltpu.VMEM((own, PAD_K), F32),
        pltpu.VMEM((full, PAD_K), F32),
        pltpu.VMEM((D, FF), BF16),
    )
    specs = [pl.BlockSpec(memory_space=pltpu.VMEM)] * 15
    specs.append(pl.BlockSpec(memory_space=pltpu.SMEM))
    return vmem_call(layer_kernel, outs, scratch, 15 * 10**9, 60 * 10**6, specs)(
        x_all, back, *tables, *places, *gain_maps, *weights, spot
    )


def run_assemble(spot, pieces):
    shape = jax.ShapeDtypeStruct
    outs = (
        shape((PAD_K, FF), BF16),
        shape((PAD_K, FF), BF16),
        shape((PAD_K, FF), BF16),
        shape((32, 2, 24, D), BF16),
    )
    specs = [pl.BlockSpec(memory_space=pltpu.SMEM)]
    specs = specs + [pl.BlockSpec(memory_space=pltpu.VMEM)] * 24
    gate, up, attn, down = vmem_call(assemble_kernel, outs, (), 0, 14 * 10**6, specs)(
        spot, *pieces
    )
    return attn, gate, up, down.reshape(FF, D)


def run_final(x_own, gain, w_pairs, d_middle, d_normed, pieces):
    outs = jax.ShapeDtypeStruct((2 * STRETCH, D), F32)
    return vmem_call(final_kernel, outs, (), 3 * 10**8, 4 * 10**6)(
        x_own, gain, w_pairs, d_middle, d_normed, *pieces
    )


def row_tables(doc_sizes, key_places, query_places):
    ends = jnp.cumsum(doc_sizes)

    def start_of(places):
        passed = places[:, None] >= ends[None, :]
        return jnp.sum(jnp.where(passed, doc_sizes[None, :], 0), axis=1)

    starts = start_of(query_places)
    allowed = (key_places[None, :] >= starts[:, None]) & (
        key_places[None, :] <= query_places[:, None]
    )
    bias = jnp.where(allowed, 0.0, MASKED).astype(F32)
    positions = key_places - start_of(key_places)
    half = HEAD // 2
    frequencies = ROPE_BASE ** (-jnp.arange(half, dtype=F32) / half)
    angles = positions.astype(F32)[:, None] * frequencies[None, :]
    return bias, jnp.cos(angles), jnp.sin(angles)


def rotary_tables(cosine, sine):
    zero = jnp.zeros_like(sine)
    return (
        jnp.concatenate([cosine] * 4, axis=1),
        jnp.concatenate([-sine, zero] * 2, axis=1),
        jnp.concatenate([zero, sine] * 2, axis=1),
    )


def ring(values, axis, step, size=4):
    return lax.ppermute(values, axis, [(i, (i + step) % size) for i in range(size)])


def swap(values):
    return lax.ppermute(values, "c", [(0, 1), (1, 0)])


def ring_z(values, step):
    def index(z):
        return (z % 2) * 4 + z // 2

    pairs = [(index(z), index((z + step) % 8)) for z in range(8)]
    return lax.ppermute(values, ("zl", "zh"), pairs)


def rolled(stack, start):
    return lax.dynamic_slice_in_dim(jnp.concatenate([stack, stack], axis=0), start, stack.shape[0], 0)


def gather_weights(shards, spot):
    w_query, w_key, w_value, w_out, w_gate, w_up, w_down, gain_attn, gain_ffn = shards
    first = spot["core"] == 0

    def halves(a_part, left, right, down):
        gains = jnp.concatenate([gain_attn, gain_ffn, jnp.zeros((252,), BF16)])[None]
        rows = jnp.concatenate([a_part, left, right], axis=1)
        rows = jnp.concatenate([rows, gains, jnp.zeros((5, 288), BF16)], axis=0)
        return jnp.concatenate([rows, down], axis=1)

    lower = halves(w_gate, w_query, w_key, w_down[:24])
    upper = halves(w_up, w_out, w_value, w_down[24:])
    keep = jnp.where(first, lower, upper)
    taken = swap(jnp.where(first, upper, lower))
    pair = jnp.concatenate(
        [jnp.where(first, keep, taken), jnp.where(first, taken, keep)], axis=1
    )
    column = [pair] + [ring_z(pair, k) for k in range(1, 8)]
    stack = jnp.stack([column[0]] + column[:0:-1])
    stack = rolled(stack, lax.rem(8 - spot["z"], 8)).reshape(4, 2, 24, 2, 360)

    def wide(part, rows):
        return jnp.transpose(part, (1, 2, 0, 3, 4)).reshape(rows, -1)

    a_block = jnp.pad(wide(stack[:, :, :18, :, :192], 36), ((0, 4), (0, 0)))
    t_block = jnp.concatenate(
        [wide(stack[:, :, :18, :, 192:264], 36), wide(stack[:, :, :18, :, 264:288], 36)], axis=1
    )
    gain_rows = jnp.pad(stack[0, :, 18, 0, :36], ((0, 2), (0, 768 - 36)))
    t_block = jnp.concatenate([t_block, gain_rows], axis=0)
    d_block = wide(stack[..., 288:], 48).reshape(2, 24, D)

    def along(block, axis):
        return [block] + [ring(block, axis, k) for k in range(1, 4)]

    a_block = jnp.concatenate(along(a_block, "y"), axis=0)
    t_block = jnp.concatenate(along(t_block, "x"), axis=0)
    d_block = jnp.concatenate(along(d_block, "x"), axis=0)
    mine_a, mine_t, mine_d = along(a_block, "x"), along(t_block, "y"), along(d_block, "y")
    other_a, other_t, other_d = ([swap(p) for p in part] for part in (mine_a, mine_t, mine_d))
    return (*mine_a, *other_a, *mine_t, *other_t, *mine_d, *other_d)


def total(parts):
    result = parts[0].astype(F32)
    for part in parts[1:]:
        result = result + part.astype(F32)
    return result


def scatter_along(chunks, axis):
    return [chunks[0]] + [ring(chunks[k], axis, 4 - k) for k in range(1, 4)]


def rows_of(parts, start, size):
    return total([part[start : start + size] for part in parts]).astype(BF16)


def reduce_grads(pieces, spot):
    first = spot["core"] == 0
    mine_a, other_a, mine_t, other_t, mine_d, other_d = (
        pieces[4 * i : 4 * i + 4] for i in range(6)
    )

    def paired(mine, other):
        return [total([m, swap(o)]).astype(BF16) for m, o in zip(mine, other)]

    def stage(mine, other, axis, size):
        received = scatter_along(paired(mine, other), axis)
        return [rows_of(received, k * size, size) for k in range(4)]

    a_parts = stage(mine_a, other_a, "x", 40)
    t_parts = stage(mine_t, other_t, "y", 40)
    d_parts = stage(mine_d, other_d, "y", 2)
    a_block = total(scatter_along(a_parts, "y")).astype(BF16)
    t_block = total(scatter_along(t_parts, "x")).astype(BF16)
    d_block = total(scatter_along(d_parts, "x")).astype(BF16)

    def narrow(part, rows, width):
        return jnp.transpose(part.reshape(2, rows, 4, 2, width), (2, 0, 1, 3, 4))

    rows = jnp.concatenate(
        [
            narrow(a_block[:36], 18, 192),
            narrow(t_block[:36, :D], 18, 72),
            narrow(t_block[:36, D:], 18, 24),
        ],
        axis=-1,
    )
    gain_rows = jnp.broadcast_to(t_block[36:38, :36][None, :, None, None], (4, 2, 1, 2, 36))
    gain_rows = jnp.pad(gain_rows, ((0, 0), (0, 0), (0, 5), (0, 0), (0, 252)))
    packets = jnp.concatenate(
        [jnp.concatenate([rows, gain_rows], axis=2), narrow(d_block, 24, 72)], axis=-1
    )
    packets = rolled(packets.reshape(8, 24, 720), spot["z"])
    received = [packets[0]] + [ring_z(packets[k], k) for k in range(1, 8)]
    summed = total(received)
    gain_stack = jnp.stack([part[18, :36] for part in [received[0]] + received[:0:-1]])
    gains = jnp.sum(rolled(gain_stack, lax.rem(8 - spot["z"], 8)).astype(F32), axis=0)
    low_half, high_half = summed[:, :360], summed[:, 360:]
    keep = jnp.where(first, low_half, high_half)
    taken = swap(jnp.where(first, high_half, low_half).astype(BF16)).astype(F32)
    lower = jnp.where(first, keep, taken)
    upper = jnp.where(first, taken, keep)
    return (
        gains[:18],
        lower[:18, 192:264],
        lower[:18, 264:288],
        upper[:18, 264:288],
        upper[:18, 192:264],
        gains[18:],
        lower[:18, :192],
        upper[:18, :192],
        jnp.concatenate([lower[:, 288:], upper[:, 288:]], axis=0),
    )


def body(
    tokens,
    lengths,
    gain_attn,
    w_query,
    w_key,
    w_value,
    w_out,
    gain_ffn,
    w_gate,
    w_up,
    w_down,
    cotangent,
):
    core, z_high, z_low = lax.axis_index("c"), lax.axis_index("zh"), lax.axis_index("zl")
    x_pos, y_pos = lax.axis_index("x"), lax.axis_index("y")
    spot = {"core": core, "z": z_high * 2 + z_low}
    spot_array = jnp.stack([core, x_pos, y_pos]).astype(jnp.int32)
    shards = (w_query, w_key, w_value, w_out, w_gate, w_up, w_down, gain_attn, gain_ffn)
    pieces = gather_weights(shards, spot)

    x_own = tokens.reshape(2 * STRETCH, D)
    x_mine = [x_own] + [ring(x_own, "zh", k) for k in range(1, 4)]
    x_parts = x_mine + [swap(part) for part in x_mine]
    x_all = jnp.concatenate(
        [part[m * STRETCH : (m + 1) * STRETCH] for m in range(2) for part in x_parts], axis=0
    )
    slot = jnp.arange(8, dtype=jnp.int32)
    holder = lax.rem(z_high + 4 - lax.rem(slot, 4), 4) * 2 + jnp.where(slot < 4, core, 1 - core)
    steps = jnp.arange(STRETCH, dtype=jnp.int32)
    key_places = (holder[:, None] * STRETCH + steps[None, :]).reshape(GROUP)
    query_places = (z_high * 2 + core) * STRETCH + steps
    made = [row_tables(lengths[m, 0], key_places, query_places) for m in range(2)]
    bias = jnp.stack([made[0][0], made[1][0]])
    tables = (bias,) + rotary_tables(
        jnp.concatenate([made[0][1], made[1][1]]), jnp.concatenate([made[0][2], made[1][2]])
    )
    places, gain_maps = placements(x_pos, y_pos)
    weights = run_assemble(spot_array, pieces)
    results = run_layer(
        x_all, cotangent.reshape(2 * STRETCH, D), tables, places, gain_maps, weights, spot_array
    )
    block_out, d_middle, d_normed, d_pairs, w_pairs, gain = results[:6]

    by_slot = d_pairs.reshape(2, 8, STRETCH, 512)
    other = swap(by_slot[:, 4:])
    joined = (by_slot[:, :4].astype(F32) + other.astype(F32)).astype(BF16)
    sent = [joined[:, k].reshape(2 * STRETCH, 512) for k in range(4)]
    pair_parts = scatter_along(sent, "zh")
    d_tokens = run_final(x_own, gain, w_pairs, d_middle, d_normed, pair_parts)
    grads = reduce_grads(results[6:], spot)
    return (
        block_out.reshape(2, STRETCH, D),
        d_tokens.reshape(2, STRETCH, D),
        *grads,
    )


def placements(x_pos, y_pos):
    feature = jnp.arange(D, dtype=jnp.int32)
    z, x, y, i = feature // 288, (feature // 72) % 4, (feature // 18) % 4, feature % 18
    x_rel, y_rel = lax.rem(x_pos + 4 - x, 4), lax.rem(y_pos + 4 - y, 4)
    start_a, start_b = (x_rel * 4 + y_rel) * BLOCK_K, (y_rel * 4 + x_rel) * BLOCK_K
    inside = z * 18 + i
    columns = jnp.arange(PAD_K, dtype=jnp.int32)
    place_a = ((start_a + inside)[:, None] == columns[None, :]).astype(BF16)
    place_b = ((start_b + inside)[:, None] == columns[None, :]).astype(BF16)
    place_bt = ((start_b + inside)[None, :] == columns[:, None]).astype(BF16)
    row_mask = ((start_b + 36 + z)[None, :] == columns[:, None]).astype(BF16)
    lanes = jnp.arange(LANES, dtype=jnp.int32)[:, None]
    lane_maps = jnp.stack([lanes == i[None, :], lanes == (i + 18)[None, :]]).astype(BF16)
    return (place_a, place_b, place_bt), (row_mask, lane_maps)


def solution(mesh):
    split = Mesh(mesh.devices.reshape(2, 4, 4, 4, 2), ("zl", "x", "y", "zh", "c"))
    rows, columns = ("zl", "x", "y"), ("zh", "c")
    everywhere = P(None, rows + columns, None)
    matrix, vector = P(rows, columns), P(rows)
    in_specs = (
        everywhere,
        P(None, rows, None),
        vector,
        matrix,
        matrix,
        matrix,
        matrix,
        vector,
        matrix,
        matrix,
        matrix,
        everywhere,
    )
    out_specs = (
        everywhere,
        everywhere,
        vector,
        matrix,
        matrix,
        matrix,
        matrix,
        vector,
        matrix,
        matrix,
        matrix,
    )
    return jax.shard_map(body, mesh=split, in_specs=in_specs, out_specs=out_specs, check_vma=False)
```

time: 1800 us -> 380 us (0.21)
  blocking collectives: 743 us -> 0 us
  waiting for transfers between devices: 715 us -> 115 us
  Pallas kernels: 0 us -> 63.7 us
  matrix products: 61.1 us -> 0 us
  starting transfers between devices: 168 us -> 132 us
  local copies, waits for them, and re-layouts: 55.7 us -> 34.2 us
  between operations: 20.6 us -> 2.01 us
    all_gather x13 -> x0, blocking collectives: 487 us -> none  [the longest x1 71.5 us: fetch_weights(): lax.all_gather(widened[2], 'dp', axis=0, tiled=True)]
    unnamed x85 -> x0, waiting for transfers between devices: 391 us -> none
    reduce_scatter x2 -> x0, waiting for transfers between devices: 324 us -> none  [reduce_grads(): lax.psum_scatter(gradients[6].astype(jnp.bfloat16), 'dp', scatter_dimensi...]
    unnamed x3 -> x0, blocking collectives: 256 us -> none
    unnamed x72 -> x0, starting transfers between devices: 168 us -> none
    ppermute x0 -> x87, starting transfers between devices: none -> 132 us  [the longest x42 61.6 us: ring(): lax.ppermute(values, axis, [(i, (i + step) % size) for i in range(size)])]
    ppermute x0 -> x87, waiting for transfers between devices: none -> 115 us  [the longest x42 104 us: ring(): lax.ppermute(values, axis, [(i, (i + step) % size) for i in range(size)])]
    pallas_call x0 -> x3, Pallas kernels: none -> 63.7 us  [the longest x1 53.6 us: run_layer(): vmem_call(layer_kernel, outs, scratch, 15 * 10 ** 9, 60 * 10 ** 6, specs)]
  transfers between devices with their start and end apart: 77 -> 87, of which waited for: 8 -> 26; matrix products, arithmetic and copies ran while one was open for 6% -> 14% of each run, Pallas kernels for 0% -> 0%
where the time goes in v1:
time: 380 us; the launch traced here: 375 us
  starting transfers between devices  132 us (35%)
  waiting for transfers between devices  115 us (30%)
  Pallas kernels  63.7 us (17%)
  local copies, waits for them, and re-layouts  34.2 us (9%)
  other arithmetic  27.9 us (7%)
    ppermute x42, waiting for transfers between devices, ring(): lax.ppermute(values, axis, [(i, (i + step) % size) for i in range(size)])  104 us
    ppermute x42, starting transfers between devices, ring(): lax.ppermute(values, axis, [(i, (i + step) % size) for i in range(size)])  61.6 us
    pallas_call x1, Pallas kernels, run_layer(): vmem_call(layer_kernel, outs, scratch, 15 * 10 ** 9, 60 * 10 ** 6, specs)  53.6 us
    ppermute x14, starting transfers between devices, ring_z(): return lax.ppermute(values, ('zl', 'zh'), pairs)  38.5 us
    ppermute x31, starting transfers between devices, swap(): return lax.ppermute(values, 'c', [(0, 1), (1, 0)])  32 us
    unnamed x151, local copies, waits for them, and re-layouts  19.9 us
  transfers between devices with their start and end apart: 87, of which 26 were waited for; matrix products, arithmetic and copies ran while one was open for 14% of the time, Pallas kernels for 0%

profile of v1, /device:TPU:1, one launch (start us, length us, event | category | flops | bytes accessed | tf_op | source)
XLA Modules:
  0.0 375.5 jit_solution(8618939501120882710)
XLA Ops:
  3.0 3.3 collective-permute-start.7
  17.7 1.9 pad_maximum_fusion.1.cos_ref
  23.3 3.0 pad_maximum_fusion.3
  29.4 4.7 %collective-permute-start.12 = (bf16[24,720]{1,0:T(8,128)(2,1)S(1)}, bf16[24,720]{1,0:T(8,128)(2,1)S(1)}, u32[]{:S(2)}, u32[]{:S(2)}) collective-permute-start(bf16[24,720]{1,0:T(8,128)(2,1)S(1)} %pad_maximum_fusion.9), channel_id=1, source_target_pairs={{0,130},{128,4},{2,132},{130,6},{4,134},{132,0},{6,128},{134,2},{1... | collective-permute-start | bytes 103688 | tf_op jit(solution)/shard_map/ppermute | solution.py:472
  35.1 3.9 %collective-permute-start.10 = (bf16[24,720]{1,0:T(8,128)(2,1)S(1)}, bf16[24,720]{1,0:T(8,128)(2,1)S(1)}, u32[]{:S(2)}, u32[]{:S(2)}) collective-permute-start(bf16[24,720]{1,0:T(8,128)(2,1)S(1)} %pad_maximum_fusion.9), channel_id=1, source_target_pairs={{0,132},{128,6},{2,134},{130,0},{4,128},{132,2},{6,130},{134,4},{1... | collective-permute-start | bytes 103688 | tf_op jit(solution)/shard_map/ppermute | solution.py:472
  39.8 2.7 collective-permute-done.8
  42.5 2.7 collective-permute-start.9
  46.2 2.8 collective-permute-start.14
  49.1 2.6 collective-permute-done.14
  53.1 2.5 collective-permute-start.27
  60.3 3.2 collective-permute-done.35
  63.5 2.7 collective-permute-start.17
  68.1 4.3 %collective-permute-done.25 = bf16[40,768]{1,0:T(8,128)(2,1)S(1)} collective-permute-done((bf16[40,768]{1,0:T(8,128)(2,1)S(1)}, bf16[40,768]{1,0:T(8,128)(2,1)S(1)}, u32[]{:S(2)}, u32[]{:S(2)}) %collective-permute-start.25) | collective-permute-done | bytes 61472 | tf_op jit(solution)/shard_map/ppermute | solution.py:460
  72.4 8.5 %collective-permute-start.3 = (bf16[256,576]{1,0:T(8,128)(2,1)S(1)}, bf16[256,576]{1,0:T(8,128)(2,1)S(1)}, u32[]{:S(2)}, u32[]{:S(2)}) collective-permute-start(bf16[256,576]{1,0:T(8,128)(2,1)S(1)} %bitcast.95), channel_id=1, source_target_pairs={{0,1},{1,0},{2,3},{3,2},{4,5},{5,4},{6,7},{7,6},{8,9},{9,8},{10,11... | collective-permute-start | bytes 884744 | tf_op jit(solution)/shard_map/ppermute | solution.py:464
  80.9 2.8 collective-permute-start.2
  85.6 2.1 collective-permute-start.40
  88.4 15.8 %collective-permute-done.1 = bf16[256,576]{1,0:T(8,128)(2,1)S(1)} collective-permute-done((bf16[256,576]{1,0:T(8,128)(2,1)S(1)}, bf16[256,576]{1,0:T(8,128)(2,1)S(1)}, u32[]{:S(2)}, u32[]{:S(2)}) %collective-permute-start.1) | collective-permute-done | bytes 294944 | tf_op jit(solution)/shard_map/ppermute | solution.py:460
  104.2 10.2 %collective-permute-start.39 = (bf16[8,24,576]{2,1,0:T(8,128)(2,1)S(1)}, bf16[8,24,576]{2,1,0:T(8,128)(2,1)S(1)}, u32[]{:S(2)}, u32[]{:S(2)}) collective-permute-start(bf16[8,24,576]{2,1,0:T(8,128)(2,1)S(1)} %constant_dynamic-update-slice_fusion.16.refs_16_), channel_id=1, source_target_pairs={{0,16},{8,24},{16,0},{24,8},{1,17},{9,25},{17,1},{25,9},{2,18},{10... | collective-permute-start | bytes 663560 | tf_op jit(solution)/shard_map/ppermute | solution.py:460
  119.4 2.3 collective-permute-start.30
  123.7 2.1 collective-permute-start.38
  126.4 15.9 %collective-permute-done.38.refs_17_ = bf16[8,24,576]{2,1,0:T(8,128)(2,1)S(1)} collective-permute-done((bf16[8,24,576]{2,1,0:T(8,128)(2,1)S(1)}, bf16[8,24,576]{2,1,0:T(8,128)(2,1)S(1)}, u32[]{:S(2)}, u32[]{:S(2)}) %collective-permute-start.38) | collective-permute-done | bytes 221216 | tf_op jit(solution)/shard_map/ppermute | solution.py:460
  149.4 5.2 %collective-permute-done.20.refs_3_ = bf16[160,1536]{1,0:T(8,128)(2,1)S(1)} collective-permute-done((bf16[160,1536]{1,0:T(8,128)(2,1)S(1)}, bf16[160,1536]{1,0:T(8,128)(2,1)S(1)}, u32[]{:S(2)}, u32[]{:S(2)}) %collective-permute-start.20) | collective-permute-done | bytes 491552 | tf_op jit(solution)/shard_map/ppermute | solution.py:460
  154.6 2.3 collective-permute-start.24
  158.6 9.1 %collective-permute-done.18.refs_1_ = bf16[160,1536]{1,0:T(8,128)(2,1)S(1)} collective-permute-done((bf16[160,1536]{1,0:T(8,128)(2,1)S(1)}, bf16[160,1536]{1,0:T(8,128)(2,1)S(1)}, u32[]{:S(2)}, u32[]{:S(2)}) %collective-permute-start.18) | collective-permute-done | bytes 491552 | tf_op jit(solution)/shard_map/ppermute | solution.py:460
  172.0 6.9 %shard_map.203 = (bf16[640,1536]{1,0:T(8,128)(2,1)}, bf16[640,1536]{1,0:T(8,128)(2,1)}, bf16[640,1536]{1,0:T(8,128)(2,1)}, bf16[32,2,24,576]{3,2,1,0:T(8,128)(2,1)}) custom-call(s32[3]{0:T(128)} %pad_add_fusion.core_ref, bf16[160,1536]{1,0:T(8,128)(2,1)} %copy-done.1, bf16[160,1536]{1,0:T(8,128)(2,1)} %copy-done.9, bf16[160,1536]{1,0:T(8,128)(2,1)} %copy-done.8, ...), custom_call_target="tpu_custom_call" | custom-call | bytes 14000000 | tf_op jit(solution)/shard_map/pallas_call | solution.py:418
  179.0 53.6 %shard_map.204 = (bf16[256,576]{1,0:T(8,128)(2,1)}, f32[256,576]{1,0:T(8,128)}, f32[256,576]{1,0:T(8,128)}, bf16[2048,512]{1,0:T(8,128)(2,1)}, bf16[576,512]{1,0...) custom-call(bf16[2048,576]{1,0:T(8,128)(2,1)} %slice_dynamic-update-, ...), custom_call_target="tpu_custom_call" | custom-call | flops 15000000512 | bytes 60000000 | tf_op jit(solution)/shard_map/pallas_call | solution.py:403
  232.5 1.9 copy.121
  235.8 1.8 fusion.35
  245.6 2.6 collective-permute-start.61
  248.2 2.7 collective-permute-done.71
  252.6 3.3 collective-permute-start.65
  256.0 3.2 collective-permute-done.75
  261.5 2.0 collective-permute-start.52
  265.2 3.9 %collective-permute-done.65 = bf16[160,768]{1,0:T(8,128)(2,1)S(1)} collective-permute-done((bf16[160,768]{1,0:T(8,128)(2,1)S(1)}, bf16[160,768]{1,0:T(8,128)(2,1)S(1)}, u32[]{:S(2)}, u32[]{:S(2)}) %collective-permute-start.65) | collective-permute-done | bytes 245792 | tf_op jit(solution)/shard_map/ppermute | solution.py:460
  280.3 2.8 collective-permute-start.67
  283.3 21.6 %collective-permute-done.68 = bf16[40,768]{1,0:T(8,128)(2,1)} collective-permute-done((bf16[40,768]{1,0:T(8,128)(2,1)}, bf16[40,768]{1,0:T(8,128)(2,1)}, u32[]{:S(2)}, u32[]{:S(2)}) %collective-permute-start.68) | collective-permute-done | bytes 61472 | tf_op jit(solution)/shard_map/ppermute | solution.py:460
  312.7 5.2 %collective-permute-done.58 = bf16[40,1536]{1,0:T(8,128)(2,1)S(1)} collective-permute-done((bf16[40,1536]{1,0:T(8,128)(2,1)S(1)}, bf16[40,1536]{1,0:T(8,128)(2,1)S(1)}, u32[]{:S(2)}, u32[]{:S(2)}) %collective-permute-start.58) | collective-permute-done | bytes 122912 | tf_op jit(solution)/shard_map/ppermute | solution.py:460
  319.4 10.7 %collective-permute-start.85 = (bf16[24,720]{1,0:T(8,128)(2,1)S(1)}, bf16[24,720]{1,0:T(8,128)(2,1)S(1)}, u32[]{:S(2)}, u32[]{:S(2)}) collective-permute-start(bf16[24,720]{1,0:T(8,128)(2,1)S(1)} %get-tuple-element.166), channel_id=1, source_target_pairs={{0,128},{128,2},{2,130},{130,4},{4,132},{132,6},{6,134},{134,0},{1... | collective-permute-start | bytes 103688 | tf_op jit(solution)/shard_map/ppermute | solution.py:472
  330.4 2.9 collective-permute-start.83
  333.3 2.7 collective-permute-start.82
  337.7 3.6 collective-permute-start.80
  342.1 2.7 collective-permute-start.47
  345.0 3.6 collective-permute-start.46
  348.8 4.0 %collective-permute-start.86 = (bf16[24,360]{1,0:T(8,128)(2,1)S(1)}, bf16[24,360]{1,0:T(8,128)(2,1)S(1)}, u32[]{:S(2)}, u32[]{:S(2)}) collective-permute-start(bf16[24,360]{1,0:T(8,128)(2,1)S(1)} %select_convert_fusion), channel_id=1, source_target_pairs={{0,1},{1,0},{2,3},{3,2},{4,5},{5,4},{6,7},{7,6},{8,9},{9,8},{10,11... | collective-permute-start | bytes 51848 | tf_op jit(solution)/shard_map/ppermute | solution.py:464
  358.4 3.0 collective-permute-done.48.refs_3_
  361.4 7.8 %collective-permute-done.46.refs_1_ = bf16[256,512]{1,0:T(8,128)(2,1)S(1)} collective-permute-done((bf16[256,512]{1,0:T(8,128)(2,1)S(1)}, bf16[256,512]{1,0:T(8,128)(2,1)S(1)}, u32[]{:S(2)}, u32[]{:S(2)}) %collective-permute-start.46) | collective-permute-done | bytes 262176 | tf_op jit(solution)/shard_map/ppermute | solution.py:460
  369.8 3.2 shard_map.205
  373.1 2.1 copy.122
  (404 shorter events, 99.4 us)
Async XLA Ops:
  3.0 24.8 %collective-permute-start.7 = (bf16[24,360]{1,0:T(8,128)(2,1)S(1)}, bf16[24,360]{1,0:T(8,128)(2,1)S(1)}, u32[]{:S(2)}, u32[]{:S(2)}) collective-permute-start(bf16[24,360]{1,0:T(8,128)(2,1)S(1)} %broadcast_select_fusion.2), channel_id=1, source_target_pairs={{0,1},{1,0},{2,3},{3,2},{4,5},{5,4},{6,7},{7,6},{8,9},{9,8},{10,11... | collective-permute-start | bytes 51848 | tf_op jit(solution)/shard_map/ppermute | solution.py:464
  28.1 20.9 %collective-permute-start.13 = (bf16[24,720]{1,0:T(8,128)(2,1)S(1)}, bf16[24,720]{1,0:T(8,128)(2,1)S(1)}, u32[]{:S(2)}, u32[]{:S(2)}) collective-permute-start(bf16[24,720]{1,0:T(8,128)(2,1)S(1)} %pad_maximum_fusion.9), channel_id=1, source_target_pairs={{0,2},{128,130},{2,4},{130,132},{4,6},{132,134},{6,0},{134,128},{1... | collective-permute-start | bytes 103688 | tf_op jit(solution)/shard_map/ppermute | solution.py:472
  29.4 19.6 %collective-permute-start.12 = (bf16[24,720]{1,0:T(8,128)(2,1)S(1)}, bf16[24,720]{1,0:T(8,128)(2,1)S(1)}, u32[]{:S(2)}, u32[]{:S(2)}) collective-permute-start(bf16[24,720]{1,0:T(8,128)(2,1)S(1)} %pad_maximum_fusion.9), channel_id=1, source_target_pairs={{0,130},{128,4},{2,132},{130,6},{4,134},{132,0},{6,128},{134,2},{1... | collective-permute-start | bytes 103688 | tf_op jit(solution)/shard_map/ppermute | solution.py:472
  34.1 14.9 %collective-permute-start.11 = (bf16[24,720]{1,0:T(8,128)(2,1)S(1)}, bf16[24,720]{1,0:T(8,128)(2,1)S(1)}, u32[]{:S(2)}, u32[]{:S(2)}) collective-permute-start(bf16[24,720]{1,0:T(8,128)(2,1)S(1)} %pad_maximum_fusion.9), channel_id=1, source_target_pairs={{0,4},{128,132},{2,6},{130,134},{4,0},{132,128},{6,2},{134,130},{1... | collective-permute-start | bytes 103688 | tf_op jit(solution)/shard_map/ppermute | solution.py:472
  35.1 13.9 %collective-permute-start.10 = (bf16[24,720]{1,0:T(8,128)(2,1)S(1)}, bf16[24,720]{1,0:T(8,128)(2,1)S(1)}, u32[]{:S(2)}, u32[]{:S(2)}) collective-permute-start(bf16[24,720]{1,0:T(8,128)(2,1)S(1)} %pad_maximum_fusion.9), channel_id=1, source_target_pairs={{0,132},{128,6},{2,134},{130,0},{4,128},{132,2},{6,130},{134,4},{1... | collective-permute-start | bytes 103688 | tf_op jit(solution)/shard_map/ppermute | solution.py:472
  53.1 14.3 %collective-permute-start.27 = (bf16[40,768]{1,0:T(8,128)(2,1)S(1)}, bf16[40,768]{1,0:T(8,128)(2,1)S(1)}, u32[]{:S(2)}, u32[]{:S(2)}) collective-permute-start(bf16[40,768]{1,0:T(8,128)(2,1)S(1)} %pad_maximum_fusion.8), channel_id=1, source_target_pairs={{0,96},{32,0},{64,32},{96,64},{1,97},{33,1},{65,33},{97,65},{2,98}... | collective-permute-start | bytes 184328 | tf_op jit(solution)/shard_map/ppermute | solution.py:460
  55.6 12.6 %collective-permute-start.26 = (bf16[40,768]{1,0:T(8,128)(2,1)S(1)}, bf16[40,768]{1,0:T(8,128)(2,1)S(1)}, u32[]{:S(2)}, u32[]{:S(2)}) collective-permute-start(bf16[40,768]{1,0:T(8,128)(2,1)S(1)} %pad_maximum_fusion.8), channel_id=1, source_target_pairs={{0,64},{32,96},{64,0},{96,32},{1,65},{33,97},{65,1},{97,33},{2,66}... | collective-permute-start | bytes 184328 | tf_op jit(solution)/shard_map/ppermute | solution.py:460
  63.5 17.4 %collective-permute-start.17 = (bf16[40,1536]{1,0:T(8,128)(2,1)S(1)}, bf16[40,1536]{1,0:T(8,128)(2,1)S(1)}, u32[]{:S(2)}, u32[]{:S(2)}) collective-permute-start(bf16[40,1536]{1,0:T(8,128)(2,1)S(1)} %pad.12), channel_id=1, source_target_pairs={{0,24},{8,0},{16,8},{24,16},{1,25},{9,1},{17,9},{25,17},{2,26},{10... | collective-permute-start | bytes 368648 | tf_op jit(solution)/shard_map/ppermute | solution.py:460
  66.2 17.5 %collective-permute-start.16 = (bf16[40,1536]{1,0:T(8,128)(2,1)S(1)}, bf16[40,1536]{1,0:T(8,128)(2,1)S(1)}, u32[]{:S(2)}, u32[]{:S(2)}) collective-permute-start(bf16[40,1536]{1,0:T(8,128)(2,1)S(1)} %pad.12), channel_id=1, source_target_pairs={{0,16},{8,24},{16,0},{24,8},{1,17},{9,25},{17,1},{25,9},{2,18},{10... | collective-permute-start | bytes 368648 | tf_op jit(solution)/shard_map/ppermute | solution.py:460
  66.7 18.3 %collective-permute-start.15 = (bf16[40,1536]{1,0:T(8,128)(2,1)S(1)}, bf16[40,1536]{1,0:T(8,128)(2,1)S(1)}, u32[]{:S(2)}, u32[]{:S(2)}) collective-permute-start(bf16[40,1536]{1,0:T(8,128)(2,1)S(1)} %pad.12), channel_id=1, source_target_pairs={{0,8},{8,16},{16,24},{24,0},{1,9},{9,17},{17,25},{25,1},{2,10},{10... | collective-permute-start | bytes 368648 | tf_op jit(solution)/shard_map/ppermute | solution.py:460
  67.4 18.2 %collective-permute-start = (bf16[256,576]{1,0:T(8,128)(2,1)S(1)}, bf16[256,576]{1,0:T(8,128)(2,1)S(1)}, u32[]{:S(2)}, u32[]{:S(2)}) collective-permute-start(bf16[256,576]{1,0:T(8,128)(2,1)S(1)} %bitcast.94), channel_id=1, source_target_pairs={{0,2},{2,4},{4,6},{6,0},{1,3},{3,5},{5,7},{7,1},{8,10},{10,12},{12... | collective-permute-start | bytes 884744 | tf_op jit(solution)/shard_map/ppermute | solution.py:460
  72.4 44.4 %collective-permute-start.3 = (bf16[256,576]{1,0:T(8,128)(2,1)S(1)}, bf16[256,576]{1,0:T(8,128)(2,1)S(1)}, u32[]{:S(2)}, u32[]{:S(2)}) collective-permute-start(bf16[256,576]{1,0:T(8,128)(2,1)S(1)} %bitcast.95), channel_id=1, source_target_pairs={{0,1},{1,0},{2,3},{3,2},{4,5},{5,4},{6,7},{7,6},{8,9},{9,8},{10,11... | collective-permute-start | bytes 884744 | tf_op jit(solution)/shard_map/ppermute | solution.py:464
  80.9 34.2 %collective-permute-start.2 = (bf16[256,576]{1,0:T(8,128)(2,1)S(1)}, bf16[256,576]{1,0:T(8,128)(2,1)S(1)}, u32[]{:S(2)}, u32[]{:S(2)}) collective-permute-start(bf16[256,576]{1,0:T(8,128)(2,1)S(1)} %bitcast.96), channel_id=1, source_target_pairs={{0,6},{2,0},{4,2},{6,4},{1,7},{3,1},{5,3},{7,5},{8,14},{10,8},{12,... | collective-permute-start | bytes 884744 | tf_op jit(solution)/shard_map/ppermute | solution.py:460
  83.8 20.4 %collective-permute-start.1 = (bf16[256,576]{1,0:T(8,128)(2,1)S(1)}, bf16[256,576]{1,0:T(8,128)(2,1)S(1)}, u32[]{:S(2)}, u32[]{:S(2)}) collective-permute-start(bf16[256,576]{1,0:T(8,128)(2,1)S(1)} %bitcast.97), channel_id=1, source_target_pairs={{0,4},{2,6},{4,0},{6,2},{1,5},{3,7},{5,1},{7,3},{8,12},{10,14},{12... | collective-permute-start | bytes 884744 | tf_op jit(solution)/shard_map/ppermute | solution.py:460
  85.0 37.4 %collective-permute-start.41 = (bf16[8,24,576]{2,1,0:T(8,128)(2,1)S(1)}, bf16[8,24,576]{2,1,0:T(8,128)(2,1)S(1)}, u32[]{:S(2)}, u32[]{:S(2)}) collective-permute-start(bf16[8,24,576]{2,1,0:T(8,128)(2,1)S(1)} %constant_dynamic-update-slice_fusion.16.refs_16_), channel_id=1, source_target_pairs={{0,1},{1,0},{2,3},{3,2},{4,5},{5,4},{6,7},{7,6},{8,9},{9,8},{10,11... | collective-permute-start | bytes 663560 | tf_op jit(solution)/shard_map/ppermute | solution.py:464
  85.6 37.1 %collective-permute-start.40 = (bf16[8,24,576]{2,1,0:T(8,128)(2,1)S(1)}, bf16[8,24,576]{2,1,0:T(8,128)(2,1)S(1)}, u32[]{:S(2)}, u32[]{:S(2)}) collective-permute-start(bf16[8,24,576]{2,1,0:T(8,128)(2,1)S(1)} %constant_dynamic-update-slice_fusion.16.refs_16_), channel_id=1, source_target_pairs={{0,24},{8,0},{16,8},{24,16},{1,25},{9,1},{17,9},{25,17},{2,26},{10... | collective-permute-start | bytes 663560 | tf_op jit(solution)/shard_map/ppermute | solution.py:460
  104.2 19.5 %collective-permute-start.39 = (bf16[8,24,576]{2,1,0:T(8,128)(2,1)S(1)}, bf16[8,24,576]{2,1,0:T(8,128)(2,1)S(1)}, u32[]{:S(2)}, u32[]{:S(2)}) collective-permute-start(bf16[8,24,576]{2,1,0:T(8,128)(2,1)S(1)} %constant_dynamic-update-slice_fusion.16.refs_16_), channel_id=1, source_target_pairs={{0,16},{8,24},{16,0},{24,8},{1,17},{9,25},{17,1},{25,9},{2,18},{10... | collective-permute-start | bytes 663560 | tf_op jit(solution)/shard_map/ppermute | solution.py:460
  118.7 23.7 %collective-permute-start.31 = (bf16[160,768]{1,0:T(8,128)(2,1)S(1)}, bf16[160,768]{1,0:T(8,128)(2,1)S(1)}, u32[]{:S(2)}, u32[]{:S(2)}) collective-permute-start(bf16[160,768]{1,0:T(8,128)(2,1)S(1)} %concatenate.100.refs_8_), channel_id=1, source_target_pairs={{0,1},{1,0},{2,3},{3,2},{4,5},{5,4},{6,7},{7,6},{8,9},{9,8},{10,11... | collective-permute-start | bytes 737288 | tf_op jit(solution)/shard_map/ppermute | solution.py:464
  119.4 23.7 %collective-permute-start.30 = (bf16[160,768]{1,0:T(8,128)(2,1)S(1)}, bf16[160,768]{1,0:T(8,128)(2,1)S(1)}, u32[]{:S(2)}, u32[]{:S(2)}) collective-permute-start(bf16[160,768]{1,0:T(8,128)(2,1)S(1)} %concatenate.100.refs_8_), channel_id=1, source_target_pairs={{0,24},{8,0},{16,8},{24,16},{1,25},{9,1},{17,9},{25,17},{2,26},{10... | collective-permute-start | bytes 737288 | tf_op jit(solution)/shard_map/ppermute | solution.py:460
  122.4 22.1 %collective-permute-start.29 = (bf16[160,768]{1,0:T(8,128)(2,1)S(1)}, bf16[160,768]{1,0:T(8,128)(2,1)S(1)}, u32[]{:S(2)}, u32[]{:S(2)}) collective-permute-start(bf16[160,768]{1,0:T(8,128)(2,1)S(1)} %concatenate.100.refs_8_), channel_id=1, source_target_pairs={{0,16},{8,24},{16,0},{24,8},{1,17},{9,25},{17,1},{25,9},{2,18},{10... | collective-permute-start | bytes 737288 | tf_op jit(solution)/shard_map/ppermute | solution.py:460
  122.8 22.8 %collective-permute-start.28 = (bf16[160,768]{1,0:T(8,128)(2,1)S(1)}, bf16[160,768]{1,0:T(8,128)(2,1)S(1)}, u32[]{:S(2)}, u32[]{:S(2)}) collective-permute-start(bf16[160,768]{1,0:T(8,128)(2,1)S(1)} %concatenate.100.refs_8_), channel_id=1, source_target_pairs={{0,8},{8,16},{16,24},{24,0},{1,9},{9,17},{17,25},{25,1},{2,10},{10... | collective-permute-start | bytes 737288 | tf_op jit(solution)/shard_map/ppermute | solution.py:460
  123.7 18.6 %collective-permute-start.38 = (bf16[8,24,576]{2,1,0:T(8,128)(2,1)S(1)}, bf16[8,24,576]{2,1,0:T(8,128)(2,1)S(1)}, u32[]{:S(2)}, u32[]{:S(2)}) collective-permute-start(bf16[8,24,576]{2,1,0:T(8,128)(2,1)S(1)} %constant_dynamic-update-slice_fusion.16.refs_16_), channel_id=1, source_target_pairs={{0,8},{8,16},{16,24},{24,0},{1,9},{9,17},{17,25},{25,1},{2,10},{10... | collective-permute-start | bytes 663560 | tf_op jit(solution)/shard_map/ppermute | solution.py:460
  142.3 12.3 %collective-permute-start.20 = (bf16[160,1536]{1,0:T(8,128)(2,1)S(1)}, bf16[160,1536]{1,0:T(8,128)(2,1)S(1)}, u32[]{:S(2)}, u32[]{:S(2)}) collective-permute-start(bf16[160,1536]{1,0:T(8,128)(2,1)S(1)} %pad_maximum_fusion.4.refs_0_), channel_id=1, source_target_pairs={{0,96},{32,0},{64,32},{96,64},{1,97},{33,1},{65,33},{97,65},{2,98}... | collective-permute-start | bytes 1474568 | tf_op jit(solution)/shard_map/ppermute | solution.py:460
  142.4 14.6 %collective-permute-start.19 = (bf16[160,1536]{1,0:T(8,128)(2,1)S(1)}, bf16[160,1536]{1,0:T(8,128)(2,1)S(1)}, u32[]{:S(2)}, u32[]{:S(2)}) collective-permute-start(bf16[160,1536]{1,0:T(8,128)(2,1)S(1)} %pad_maximum_fusion.4.refs_0_), channel_id=1, source_target_pairs={{0,64},{32,96},{64,0},{96,32},{1,65},{33,97},{65,1},{97,33},{2,66}... | collective-permute-start | bytes 1474568 | tf_op jit(solution)/shard_map/ppermute | solution.py:460
  143.1 24.5 %collective-permute-start.18 = (bf16[160,1536]{1,0:T(8,128)(2,1)S(1)}, bf16[160,1536]{1,0:T(8,128)(2,1)S(1)}, u32[]{:S(2)}, u32[]{:S(2)}) collective-permute-start(bf16[160,1536]{1,0:T(8,128)(2,1)S(1)} %pad_maximum_fusion.4.refs_0_), channel_id=1, source_target_pairs={{0,32},{32,64},{64,96},{96,0},{1,33},{33,65},{65,97},{97,1},{2,34}... | collective-permute-start | bytes 1474568 | tf_op jit(solution)/shard_map/ppermute | solution.py:460
  148.2 21.0 %collective-permute-start.33 = (bf16[160,768]{1,0:T(8,128)(2,1)S(1)}, bf16[160,768]{1,0:T(8,128)(2,1)S(1)}, u32[]{:S(2)}, u32[]{:S(2)}) collective-permute-start(bf16[160,768]{1,0:T(8,128)(2,1)S(1)} %collective-permute-done.29.refs_10_), channel_id=1, source_target_pairs={{0,1},{1,0},{2,3},{3,2},{4,5},{5,4},{6,7},{7,6},{8,9},{9,8},{10,11... | collective-permute-start | bytes 737288 | tf_op jit(solution)/shard_map/ppermute | solution.py:464
  149.3 21.5 %collective-permute-start.21 = (bf16[160,1536]{1,0:T(8,128)(2,1)S(1)}, bf16[160,1536]{1,0:T(8,128)(2,1)S(1)}, u32[]{:S(2)}, u32[]{:S(2)}) collective-permute-start(bf16[160,1536]{1,0:T(8,128)(2,1)S(1)} %pad_maximum_fusion.4.refs_0_), channel_id=1, source_target_pairs={{0,1},{1,0},{2,3},{3,2},{4,5},{5,4},{6,7},{7,6},{8,9},{9,8},{10,11... | collective-permute-start | bytes 1474568 | tf_op jit(solution)/shard_map/ppermute | solution.py:464
  154.6 16.2 %collective-permute-start.24 = (bf16[160,1536]{1,0:T(8,128)(2,1)S(1)}, bf16[160,1536]{1,0:T(8,128)(2,1)S(1)}, u32[]{:S(2)}, u32[]{:S(2)}) collective-permute-start(bf16[160,1536]{1,0:T(8,128)(2,1)S(1)} %collective-permute-done.20.refs_3_), channel_id=1, source_target_pairs={{0,1},{1,0},{2,3},{3,2},{4,5},{5,4},{6,7},{7,6},{8,9},{9,8},{10,11... | collective-permute-start | bytes 1474568 | tf_op jit(solution)/shard_map/ppermute | solution.py:464
  156.9 13.9 %collective-permute-start.23 = (bf16[160,1536]{1,0:T(8,128)(2,1)S(1)}, bf16[160,1536]{1,0:T(8,128)(2,1)S(1)}, u32[]{:S(2)}, u32[]{:S(2)}) collective-permute-start(bf16[160,1536]{1,0:T(8,128)(2,1)S(1)} %collective-permute-done.19.refs_2_), channel_id=1, source_target_pairs={{0,1},{1,0},{2,3},{3,2},{4,5},{5,4},{6,7},{7,6},{8,9},{9,8},{10,11... | collective-permute-start | bytes 1474568 | tf_op jit(solution)/shard_map/ppermute | solution.py:464
  234.4 11.2 %collective-permute-start.59 = (bf16[160,768]{1,0:T(8,128)(2,1)}, bf16[160,768]{1,0:T(8,128)(2,1)S(1)}, u32[]{:S(2)}, u32[]{:S(2)}) collective-permute-start(bf16[160,768]{1,0:T(8,128)(2,1)} %get-tuple-element.64), channel_id=1, source_target_pairs={{0,1},{1,0},{2,3},{3,2},{4,5},{5,4},{6,7},{7,6},{8,9},{9,8},{10,11... | collective-permute-start | bytes 737288 | tf_op jit(solution)/shard_map/ppermute | solution.py:464
  243.4 27.6 %collective-permute-start.50 = (bf16[160,1536]{1,0:T(8,128)(2,1)S(1)}, bf16[160,1536]{1,0:T(8,128)(2,1)S(1)}, u32[]{:S(2)}, u32[]{:S(2)}) collective-permute-start(bf16[160,1536]{1,0:T(8,128)(2,1)S(1)} %copy-done.53), channel_id=1, source_target_pairs={{0,1},{1,0},{2,3},{3,2},{4,5},{5,4},{6,7},{7,6},{8,9},{9,8},{10,11... | collective-permute-start | bytes 1474568 | tf_op jit(solution)/shard_map/ppermute | solution.py:464
  244.3 14.9 %collective-permute-start.75 = (bf16[8,24,576]{2,1,0:T(8,128)(2,1)S(1)}, bf16[8,24,576]{2,1,0:T(8,128)(2,1)S(1)}, u32[]{:S(2)}, u32[]{:S(2)}) collective-permute-start(bf16[8,24,576]{2,1,0:T(8,128)(2,1)S(1)} %add_convert_fusion.6), channel_id=1, source_target_pairs={{0,8},{8,16},{16,24},{24,0},{1,9},{9,17},{17,25},{25,1},{2,10},{10... | collective-permute-start | bytes 663560 | tf_op jit(solution)/shard_map/ppermute | solution.py:460
  245.6 15.9 %collective-permute-start.61 = (bf16[160,768]{1,0:T(8,128)(2,1)S(1)}, bf16[160,768]{1,0:T(8,128)(2,1)S(1)}, u32[]{:S(2)}, u32[]{:S(2)}) collective-permute-start(bf16[160,768]{1,0:T(8,128)(2,1)S(1)} %add_convert_fusion.12), channel_id=1, source_target_pairs={{0,24},{8,0},{16,8},{24,16},{1,25},{9,1},{17,9},{25,17},{2,26},{10... | collective-permute-start | bytes 737288 | tf_op jit(solution)/shard_map/ppermute | solution.py:460
  250.9 12.6 %collective-permute-start.63 = (bf16[160,768]{1,0:T(8,128)(2,1)S(1)}, bf16[160,768]{1,0:T(8,128)(2,1)S(1)}, u32[]{:S(2)}, u32[]{:S(2)}) collective-permute-start(bf16[160,768]{1,0:T(8,128)(2,1)S(1)} %add_convert_fusion.11), channel_id=1, source_target_pairs={{0,16},{8,24},{16,0},{24,8},{1,17},{9,25},{17,1},{25,9},{2,18},{10... | collective-permute-start | bytes 737288 | tf_op jit(solution)/shard_map/ppermute | solution.py:460
  252.6 16.5 %collective-permute-start.65 = (bf16[160,768]{1,0:T(8,128)(2,1)S(1)}, bf16[160,768]{1,0:T(8,128)(2,1)S(1)}, u32[]{:S(2)}, u32[]{:S(2)}) collective-permute-start(bf16[160,768]{1,0:T(8,128)(2,1)S(1)} %add_convert_fusion.10), channel_id=1, source_target_pairs={{0,8},{8,16},{16,24},{24,0},{1,9},{9,17},{17,25},{25,1},{2,10},{10... | collective-permute-start | bytes 737288 | tf_op jit(solution)/shard_map/ppermute | solution.py:460
  259.2 17.4 %collective-permute-start.49 = (bf16[160,1536]{1,0:T(8,128)(2,1)S(1)}, bf16[160,1536]{1,0:T(8,128)(2,1)S(1)}, u32[]{:S(2)}, u32[]{:S(2)}) collective-permute-start(bf16[160,1536]{1,0:T(8,128)(2,1)S(1)} %copy-done.50), channel_id=1, source_target_pairs={{0,1},{1,0},{2,3},{3,2},{4,5},{5,4},{6,7},{7,6},{8,9},{9,8},{10,11... | collective-permute-start | bytes 1474568 | tf_op jit(solution)/shard_map/ppermute | solution.py:464
  276.6 30.2 %collective-permute-start.51 = (bf16[160,1536]{1,0:T(8,128)(2,1)}, bf16[160,1536]{1,0:T(8,128)(2,1)}, u32[]{:S(2)}, u32[]{:S(2)}) collective-permute-start(bf16[160,1536]{1,0:T(8,128)(2,1)} %add_convert_fusion.3), channel_id=1, source_target_pairs={{0,96},{32,0},{64,32},{96,64},{1,97},{33,1},{65,33},{97,65},{2,98}... | collective-permute-start | bytes 1474568 | tf_op jit(solution)/shard_map/ppermute | solution.py:460
  277.4 29.3 %collective-permute-start.53 = (bf16[160,1536]{1,0:T(8,128)(2,1)}, bf16[160,1536]{1,0:T(8,128)(2,1)}, u32[]{:S(2)}, u32[]{:S(2)}) collective-permute-start(bf16[160,1536]{1,0:T(8,128)(2,1)} %add_convert_fusion.2), channel_id=1, source_target_pairs={{0,64},{32,96},{64,0},{96,32},{1,65},{33,97},{65,1},{97,33},{2,66}... | collective-permute-start | bytes 1474568 | tf_op jit(solution)/shard_map/ppermute | solution.py:460
  279.0 27.8 %collective-permute-start.55 = (bf16[160,1536]{1,0:T(8,128)(2,1)}, bf16[160,1536]{1,0:T(8,128)(2,1)}, u32[]{:S(2)}, u32[]{:S(2)}) collective-permute-start(bf16[160,1536]{1,0:T(8,128)(2,1)} %add_convert_fusion.1), channel_id=1, source_target_pairs={{0,32},{32,64},{64,96},{96,0},{1,33},{33,65},{65,97},{97,1},{2,34}... | collective-permute-start | bytes 1474568 | tf_op jit(solution)/shard_map/ppermute | solution.py:460
  279.9 25.0 %collective-permute-start.68 = (bf16[40,768]{1,0:T(8,128)(2,1)}, bf16[40,768]{1,0:T(8,128)(2,1)}, u32[]{:S(2)}, u32[]{:S(2)}) collective-permute-start(bf16[40,768]{1,0:T(8,128)(2,1)} %get-tuple-element.164), channel_id=1, source_target_pairs={{0,32},{32,64},{64,96},{96,0},{1,33},{33,65},{65,97},{97,1},{2,34}... | collective-permute-start | bytes 184328 | tf_op jit(solution)/shard_map/ppermute | solution.py:460
  280.3 25.1 %collective-permute-start.67 = (bf16[40,768]{1,0:T(8,128)(2,1)S(1)}, bf16[40,768]{1,0:T(8,128)(2,1)}, u32[]{:S(2)}, u32[]{:S(2)}) collective-permute-start(bf16[40,768]{1,0:T(8,128)(2,1)S(1)} %get-tuple-element.165), channel_id=1, source_target_pairs={{0,64},{32,96},{64,0},{96,32},{1,65},{33,97},{65,1},{97,33},{2,66}... | collective-permute-start | bytes 184328 | tf_op jit(solution)/shard_map/ppermute | solution.py:460
  304.9 25.2 %collective-permute-start.45 = (bf16[2,4,128,512]{3,2,0,1:T(8,128)(2,1)}, bf16[2,4,128,512]{3,2,0,1:T(8,128)(2,1)S(1)}, u32[]{:S(2)}, u32[]{:S(2)}) collective-permute-start(bf16[2,4,128,512]{3,2,0,1:T(8,128)(2,1)} %copy.125), channel_id=1, source_target_pairs={{0,1},{1,0},{2,3},{3,2},{4,5},{5,4},{6,7},{7,6},{8,9},{9,8},{10,11... | collective-permute-start | bytes 3145736 | tf_op jit(solution)/shard_map/ppermute | solution.py:464
  319.4 18.2 %collective-permute-start.85 = (bf16[24,720]{1,0:T(8,128)(2,1)S(1)}, bf16[24,720]{1,0:T(8,128)(2,1)S(1)}, u32[]{:S(2)}, u32[]{:S(2)}) collective-permute-start(bf16[24,720]{1,0:T(8,128)(2,1)S(1)} %get-tuple-element.166), channel_id=1, source_target_pairs={{0,128},{128,2},{2,130},{130,4},{4,132},{132,6},{6,134},{134,0},{1... | collective-permute-start | bytes 103688 | tf_op jit(solution)/shard_map/ppermute | solution.py:472
  330.4 11.7 %collective-permute-start.83 = (bf16[24,720]{1,0:T(8,128)(2,1)S(1)}, bf16[24,720]{1,0:T(8,128)(2,1)S(1)}, u32[]{:S(2)}, u32[]{:S(2)}) collective-permute-start(bf16[24,720]{1,0:T(8,128)(2,1)S(1)} %get-tuple-element.168), channel_id=1, source_target_pairs={{0,130},{128,4},{2,132},{130,6},{4,134},{132,0},{6,128},{134,2},{1... | collective-permute-start | bytes 103688 | tf_op jit(solution)/shard_map/ppermute | solution.py:472
  333.3 11.5 %collective-permute-start.82 = (bf16[24,720]{1,0:T(8,128)(2,1)S(1)}, bf16[24,720]{1,0:T(8,128)(2,1)S(1)}, u32[]{:S(2)}, u32[]{:S(2)}) collective-permute-start(bf16[24,720]{1,0:T(8,128)(2,1)S(1)} %get-tuple-element.169), channel_id=1, source_target_pairs={{0,4},{128,132},{2,6},{130,134},{4,0},{132,128},{6,2},{134,130},{1... | collective-permute-start | bytes 103688 | tf_op jit(solution)/shard_map/ppermute | solution.py:472
  342.1 16.3 %collective-permute-start.47 = (bf16[256,512]{1,0:T(8,128)(2,1)S(1)}, bf16[256,512]{1,0:T(8,128)(2,1)S(1)}, u32[]{:S(2)}, u32[]{:S(2)}) collective-permute-start(bf16[256,512]{1,0:T(8,128)(2,1)S(1)} %bitcast.110), channel_id=1, source_target_pairs={{0,4},{2,6},{4,0},{6,2},{1,5},{3,7},{5,1},{7,3},{8,12},{10,14},{12... | collective-permute-start | bytes 786440 | tf_op jit(solution)/shard_map/ppermute | solution.py:460
  344.8 16.5 %collective-permute-start.48 = (bf16[256,512]{1,0:T(8,128)(2,1)S(1)}, bf16[256,512]{1,0:T(8,128)(2,1)S(1)}, u32[]{:S(2)}, u32[]{:S(2)}) collective-permute-start(bf16[256,512]{1,0:T(8,128)(2,1)S(1)} %bitcast.109), channel_id=1, source_target_pairs={{0,2},{2,4},{4,6},{6,0},{1,3},{3,5},{5,7},{7,1},{8,10},{10,12},{12... | collective-permute-start | bytes 786440 | tf_op jit(solution)/shard_map/ppermute | solution.py:460
  345.0 24.2 %collective-permute-start.46 = (bf16[256,512]{1,0:T(8,128)(2,1)S(1)}, bf16[256,512]{1,0:T(8,128)(2,1)S(1)}, u32[]{:S(2)}, u32[]{:S(2)}) collective-permute-start(bf16[256,512]{1,0:T(8,128)(2,1)S(1)} %bitcast.108), channel_id=1, source_target_pairs={{0,6},{2,0},{4,2},{6,4},{1,7},{3,1},{5,3},{7,5},{8,14},{10,8},{12,... | collective-permute-start | bytes 786440 | tf_op jit(solution)/shard_map/ppermute | solution.py:460
  (96 other events, 1208.0 us)
